TPU v7x, 128 devices: a whole 4x4x4 slice. The times are simulated.
128 devices in a mesh: row: 8 (over x_lo, y), col: 16 (over z, x_hi, core).
Axes of the slice: x: 4 (x_hi: 2, x_lo: 2; x = x_hi * 2 + x_lo), y: 4, z: 4, core: 2. Of those that a mesh axis runs over, the one named last changes fastest.
Arguments:
- voltages: bfloat16 [262144, 1024], P(('row', 'col')), may hold values from -24 to 24
- filter_taps: float32 [4, 512], replicated, may hold values from -3 to 3
Outputs:
- visibilities: bfloat16 [256, 2, 1024, 1024], P(('row', 'col'))
All inputs are finite; a program needn't handle non-finite values.
Results may differ from a plain program's by a relative error of at most 0.0072.
Values may be sent and summed in bfloat16 or wider, within the bound.
A program may use at most 64 MiB of HBM per device.

v0:
```python
import jax
import jax.numpy as jnp
from jax import lax
from jax.sharding import PartitionSpec as P


def from_behind(block, axis, distance):
    devices = range(lax.axis_size(axis))
    route = [(i - distance, i) for i in devices if i - distance in devices]
    return lax.ppermute(block, axis, route)


def fourier_table(points):
    rows = jnp.arange(points // 2, dtype=jnp.int32)[:, None]
    cols = jnp.arange(points, dtype=jnp.int32)[None, :]
    phase = (rows * cols % points).astype(jnp.float32) * (2.0 * jnp.pi / points)
    scale = 1.0 / jnp.sqrt(jnp.float32(points))
    table = jnp.concatenate([jnp.cos(phase), -jnp.sin(phase)], axis=0) * scale
    return table.astype(jnp.bfloat16)


def shards(voltages, filter_taps):
    tap_count, points = filter_taps.shape
    inputs = voltages.shape[1]
    local_frames = voltages.shape[0] // points
    tail = voltages[(local_frames - tap_count + 1) * points :, :]
    history = from_behind(tail, ("row", "col"), 1)
    joined = jnp.concatenate([history, voltages], axis=0).reshape(
        local_frames + tap_count - 1, points, inputs
    )
    filtered = jnp.zeros((local_frames, points, inputs), jnp.float32)
    for tap_index in range(tap_count):
        filtered = filtered + filter_taps[tap_index][None, :, None] * joined[
            tap_index : tap_index + local_frames
        ].astype(jnp.float32)
    filtered = filtered.astype(jnp.bfloat16)
    table = fourier_table(points)
    spectra = jnp.einsum("cn,fns->cfs", table, filtered, preferred_element_type=jnp.float32).astype(
        jnp.bfloat16
    )
    spectra = spectra.reshape(2, points // 2, local_frames, inputs)
    gathered = lax.all_to_all(spectra, ("row", "col"), split_axis=1, concat_axis=2, tiled=True)
    total_spectra = gathered.shape[2]
    stacked = jnp.concatenate([gathered[0], gathered[1]], axis=1)
    rotated = jnp.concatenate([gathered[1], -gathered[0]], axis=1)
    real_part = jnp.einsum("jta,jtb->jab", stacked, stacked, preferred_element_type=jnp.float32)
    imag_part = jnp.einsum("jta,jtb->jab", rotated, stacked, preferred_element_type=jnp.float32)
    both = jnp.stack([real_part, imag_part], axis=1) * (1.0 / total_spectra)
    return both.astype(jnp.bfloat16)


def solution(mesh):
    placed = (P(("row", "col"), None), P())
    return jax.shard_map(
        shards,
        mesh=mesh,
        in_specs=placed,
        out_specs=P(("row", "col"), None, None, None),
        check_vma=False,
    )
```

profile of v0, /device:TPU:1, one launch (start us, length us, event | category | flops | bytes accessed | tf_op | source)
XLA Modules:
  0.0 156.5 jit_solution(877728389242843552)
XLA Ops:
  0.0 2.2 %slice.40 = bf16[1536,1024]{1,0:T(8,128)(2,1)S(1)} slice(bf16[2048,1024]{1,0:T(8,128)(2,1)} %param.2), slice={[512:2048], [0:1024]} | slice | bytes 6291456 | tf_op jit(solution)/shard_map/slice | solution.py:26
  2.2 0.0 copy-start
  2.2 6.3 %collective-permute-start = (bf16[1536,1024]{1,0:T(8,128)(2,1)S(1)}, bf16[1536,1024]{1,0:T(8,128)(2,1)S(1)}, u32[]{:S(2)}, u32[]{:S(2)}) collective-permute-start(bf16[1536,1024]{1,0:T(8,128)(2,1)S(1)} %slice.40), channel_id=1, source_target_pairs={{0,1},{1,2},{2,3},{3,4},{4,5},{5,6},{6,7},{7,8},{8,9},{9,10},{10,1... | collective-permute-start | bytes 9437192 | tf_op jit(solution)/shard_map/ppermute | solution.py:10
  8.5 2.1 %sine_negate_fusion = (f32[256,512]{1,0:T(8,128)S(1)}, f32[256,512]{1,0:T(8,128)S(1)}) fusion(), kind=kLoop, calls=%fused_computation.33 | loop fusion | flops 1966080 | bytes 1048576 | tf_op jit(solution)/shard_map/neg | solution.py:18
  10.6 0.0 copy-done.4
  10.6 32.1 %collective-permute-done = bf16[1536,1024]{1,0:T(8,128)(2,1)S(1)} collective-permute-done((bf16[1536,1024]{1,0:T(8,128)(2,1)S(1)}, bf16[1536,1024]{1,0:T(8,128)(2,1)S(1)}, u32[]{:S(2)}, u32[]{:S(2)}) %collective-permute-start) | collective-permute-done | bytes 3145760 | tf_op jit(solution)/shard_map/ppermute | solution.py:10
  42.7 0.3 constant_dynamic-update-slice_fusion.1
  43.1 0.4 constant_dynamic-update-slice_fusion
  43.5 1.5 fusion.35
  45.0 5.9 %fusion.18 = bf16[512,4,1024]{2,0,1:T(8,128)(2,1)} fusion(bf16[4,512,1024]{2,1,0:T(8,128)(2,1)S(1)} %bitcast.29, bf16[4,512,1024]{2,1,0:T(8,128)(2,1)S(1)} %bitcast.32, bf16[4,512,1024]{2,1,0:T(8,128)(2,1)S(1)} %bitcast.33, bf16[4,512,1024]{2,1,0:T(8,128)(2,1)S(1)} %bitcast.31, f32[512]{0:T(512)S(1)} %bitcast.36, f32[512]{0:T(512)S(1)} %bitcast.37, ...), kind=kOutput, calls=%fused_computation.22 | convolution fusion | flops 2175533056 | bytes 22028288 | tf_op jit(solution)/shard_map/cn,fns->cfs/dot_general | solution.py:38
  50.9 6.6 %copy.7 = bf16[2,256,4,1024]{3,0,2,1:T(2,128)(2,1)S(1)} copy(bf16[2,256,4,1024]{3,1,0,2:T(8,128)(2,1)} %bitcast.30) | data formatting | bytes 8388608 | tf_op jit(solution)/shard_map/reshape | solution.py:41
  57.4 64.6 %all_to_all.15 = bf16[2,256,4,1024]{3,0,2,1:T(2,128)(2,1)S(1)} all-to-all(bf16[2,256,4,1024]{3,0,2,1:T(2,128)(2,1)S(1)} %copy.7), channel_id=1, replica_groups=mesh['row'=8,'col'=16] {'row','col'}, dimensions={1} | all-to-all | bytes 8388608 | tf_op jit(solution)/shard_map/all_to_all | solution.py:42
  122.0 1.6 %copy.15 = bf16[2,128,2,4,1024]{4,3,1,2,0:T(4,128)(2,1)S(1)} copy(bf16[2,128,2,4,1024]{4,0,3,2,1:T(2,128)(2,1)S(1)} %bitcast.28) | data formatting | bytes 8388608 | tf_op jit(solution)/shard_map/all_to_all | solution.py:42
  123.7 2.5 %fusion.36 = (bf16[1,2,128,4,1024]{4,3,2,1,0:T(4,128)(2,1)S(1)}, bf16[1,2,128,4,1024]{4,3,2,1,0:T(4,128)(2,1)}) fusion(bf16[2,2,128,4,1024]{4,3,2,1,0:T(4,128)(2,1)S(1)} %bitcast.27), kind=kLoop, calls=%fused_computation.46 | loop fusion | bytes 8388608 | tf_op jit(solution)/shard_map/slice | solution.py:44
  126.1 2.0 %squeeze.9 = bf16[2,512,1024]{2,1,0:T(8,128)(2,1)} reshape(bf16[1,2,128,4,1024]{4,3,2,1,0:T(4,128)(2,1)S(1)} %get-tuple-element.8) | data formatting | bytes 4194304 | tf_op jit(solution)/shard_map/squeeze | solution.py:44
  128.2 2.5 %squeeze.8 = bf16[2,512,1024]{2,1,0:T(8,128)(2,1)S(1)} reshape(bf16[1,2,128,4,1024]{4,3,2,1,0:T(4,128)(2,1)} %get-tuple-element.9) | data formatting | bytes 4194304 | tf_op jit(solution)/shard_map/squeeze | solution.py:44
  130.7 2.0 %fusion.37 = (bf16[2,512,1024]{2,1,0:T(8,128)(2,1)}, bf16[2,1024,1024]{2,1,0:T(8,128)(2,1)S(1)}) fusion(bf16[2,512,1024]{2,1,0:T(8,128)(2,1)S(1)} %squeeze.8), kind=kLoop, calls=%fused_computation.47 | loop fusion | flops 3145727 | bytes 6291456 | tf_op jit(solution)/shard_map/neg | solution.py:45
  132.7 0.0 copy-done.1
  132.7 0.2 constant_dynamic-update-slice_fusion.2
  132.9 0.0 copy-start.3
  132.9 4.7 %convolution_bitcast_fusion = f32[2,1,1024,1024]{3,2,0,1:T(8,128)S(1)} fusion(bf16[2,1024,1024]{2,1,0:T(8,128)(2,1)S(1)} %constant_dynamic-update-slice_fusion.2), kind=kOutput, calls=%fused_computation.21 | convolution fusion | flops 4294967296 | bytes 12582912 | tf_op jit(solution)/shard_map/jta,jtb->jab/dot_general | solution.py:46
  137.7 6.6 %fusion.15 = f32[2,1,1024,1024]{3,2,0,1:T(8,128)S(1)} fusion(bf16[2,1024,1024]{2,1,0:T(8,128)(2,1)} %copy-done.3, bf16[2,512,1024]{2,1,0:T(8,128)(2,1)S(1)} %copy-done.2, bf16[2,512,1024]{2,1,0:T(8,128)(2,1)S(1)} %copy-done.1), kind=kOutput, calls=%fused_computation.20 | convolution fusion | flops 4303355904 | bytes 16777216 | tf_op jit(solution)/shard_map/jta,jtb->jab/dot_general | solution.py:47
  144.2 4.5 %fusion = bf16[2,2,1024,1024]{3,2,0,1:T(8,128)(2,1)} fusion(f32[2,1,1024,1024]{3,2,0,1:T(8,128)S(1)} %fusion.15, f32[2,1,1024,1024]{3,2,0,1:T(8,128)S(1)} %convolution_bitcast_fusion), kind=kLoop, calls=%fused_computation.1 | loop fusion | flops 12582912 | bytes 25165824 | tf_op jit(solution)/shard_map/convert_element_type | solution.py:49
  148.8 7.8 %copy.11 = bf16[2,2,1024,1024]{3,2,1,0:T(8,128)(2,1)} copy(bf16[2,2,1024,1024]{3,2,0,1:T(8,128)(2,1)} %fusion) | data formatting | bytes 16777216 | tf_op jit(solution)/shard_map/convert_element_type | solution.py:49
  (7 shorter events, 0.0 us)
Async XLA Ops:
  0.0 10.6 %copy-start.4 = (f32[4,512]{1,0:T(4,128)S(1)}, f32[4,512]{1,0:T(4,128)}, u32[]{:S(2)}) copy-start(f32[4,512]{1,0:T(4,128)} %param.3) | copy-start | bytes 24580
  2.2 40.8 %copy-start = (bf16[2048,1024]{1,0:T(8,128)(2,1)S(1)}, bf16[2048,1024]{1,0:T(8,128)(2,1)}, u32[]{:S(2)}) copy-start(bf16[2048,1024]{1,0:T(8,128)(2,1)} %param.2) | copy-start | bytes 12582916
  2.2 40.5 %collective-permute-start = (bf16[1536,1024]{1,0:T(8,128)(2,1)S(1)}, bf16[1536,1024]{1,0:T(8,128)(2,1)S(1)}, u32[]{:S(2)}, u32[]{:S(2)}) collective-permute-start(bf16[1536,1024]{1,0:T(8,128)(2,1)S(1)} %slice.40), channel_id=1, source_target_pairs={{0,1},{1,2},{2,3},{3,4},{4,5},{5,6},{6,7},{7,8},{8,9},{9,10},{10,1... | collective-permute-start | bytes 9437192 | tf_op jit(solution)/shard_map/ppermute | solution.py:10
  130.7 2.0 %copy-start.1 = (bf16[2,512,1024]{2,1,0:T(8,128)(2,1)S(1)}, bf16[2,512,1024]{2,1,0:T(8,128)(2,1)}, u32[]{:S(2)}) copy-start(bf16[2,512,1024]{2,1,0:T(8,128)(2,1)} %squeeze.9) | copy-start | bytes 6291460
  132.9 4.7 %copy-start.3 = (bf16[2,1024,1024]{2,1,0:T(8,128)(2,1)}, bf16[2,1024,1024]{2,1,0:T(8,128)(2,1)S(1)}, u32[]{:S(2)}) copy-start(bf16[2,1024,1024]{2,1,0:T(8,128)(2,1)S(1)} %constant_dynamic-update-slice_fusion.2) | copy-start | bytes 12582916
  132.9 4.7 %copy-start.2 = (bf16[2,512,1024]{2,1,0:T(8,128)(2,1)S(1)}, bf16[2,512,1024]{2,1,0:T(8,128)(2,1)}, u32[]{:S(2)}) copy-start(bf16[2,512,1024]{2,1,0:T(8,128)(2,1)} %get-tuple-element.10) | copy-start | bytes 6291460
where the time goes:
time: 157 us
  blocking collectives  64.6 us (41%)
  waiting for transfers between devices  32.1 us (20%)
  local copies, waits for them, and re-layouts  27.6 us (18%)
  matrix products  17.2 us (11%)
  other arithmetic  8.62 us (5%)
  starting transfers between devices  6.31 us (4%)
    all_to_all x1, blocking collectives, shards(): lax.all_to_all(spectra, ('row', 'col'), split_axis=1, concat_axis=2, tile...  64.6 us
    ppermute x1, waiting for transfers between devices, from_behind(): return lax.ppermute(block, axis, route)  32.1 us
    convert_element_type x1, local copies, waits for them, and re-layouts, shards(): return both.astype(jnp.bfloat16)  7.76 us
    reshape x1, local copies, waits for them, and re-layouts, shards(): spectra = spectra.reshape(2, points // 2, local_frames, inputs)  6.58 us
    dot_general x1, matrix products, shards(): jnp.einsum('jta,jtb->jab', rotated, stacked, preferred_element_type=jnp.f...  6.58 us
    ppermute x1, starting transfers between devices, from_behind(): return lax.ppermute(block, axis, route)  6.31 us
    dot_general x1, matrix products, shards(): jnp.einsum('cn,fns->cfs', table, filtered, preferred_element_type=jnp.flo...  5.88 us
    dot_general x1, matrix products, shards(): jnp.einsum('jta,jtb->jab', stacked, stacked, preferred_element_type=jnp.f...  4.72 us
  transfers between devices with their start and end apart: 1, of which 1 were waited for; matrix products, arithmetic and copies ran while one was open for 1% of the time, Pallas kernels for 0%

commit v1 on v0

v1 whole, which is shorter than its diff:
```python
import itertools

import jax
import jax.numpy as jnp
import numpy as np
from jax import lax
from jax.experimental import pallas as pl
from jax.experimental.pallas import tpu as pltpu
from jax.sharding import PartitionSpec as P

MESH = pl.DeviceIdType.MESH
DEVICES = 128
POINTS = 512
TAPS = 4
SPECTRA = 512
FRAMES = 8
REACH = FRAMES + TAPS - 1
HALF = 512
LANES = 128
GROUPS = HALF // LANES
TAIL = (TAPS - 1) * LANES
WIDE = 2 * HALF + TAIL


def orbit(offset):
    found = set()
    for turn in range(3):
        turned = offset[turn:] + offset[:turn]
        found.add(turned)
        found.add(tuple((-step) % 4 for step in turned))
    return tuple(sorted(found))


def send_order():
    hops = lambda group: sum(min(step, 4 - step) for step in group[0])
    groups = {orbit(offset) for offset in itertools.product(range(4), repeat=3)}
    ordered = []
    for group in sorted(sorted(groups), key=hops, reverse=True):
        for core in (0, 1):
            ordered += [offset + (core,) for offset in group]
    return [offset for offset in ordered if any(offset)]


ORDER = send_order()


def coordinates():
    row, col = lax.axis_index("row"), lax.axis_index("col")
    return ((col // 2) % 2) * 2 + row // 4, row % 4, col // 4, col % 2


def partner(offset):
    place = coordinates()
    x, y, z = ((own + step) % 4 for own, step in zip(place[:3], offset[:3]))
    core = (place[3] + offset[3]) % 2
    return (x % 2) * 4 + y, z * 4 + (x // 2) * 2 + core


def fourier_rows():
    turns = np.arange(POINTS // 2)[:, None] * np.arange(POINTS)[None, :] % POINTS
    phase = turns.astype(np.float32) * np.float32(2.0 * np.pi / POINTS)
    scale = np.float32(1.0) / np.sqrt(np.float32(POINTS))
    table = np.stack([np.cos(phase), -np.sin(phase)], axis=1) * scale
    return table.reshape(POINTS, POINTS).astype(jnp.bfloat16)


def spread(
    volt_ref, taps_ref, table_ref, out_ref,
    frames, weights, filtered, main, tails, outbox, inbox, lifted, added,
    near_sem, pair_send, pair_recv, send_sem, recv_sem, own_sem,
):
    row, col = lax.axis_index("row"), lax.axis_index("col")
    me = row * 16 + col
    core = col % 2
    barrier = pltpu.get_barrier_semaphore()
    for offset in ORDER:
        pl.semaphore_signal(barrier, inc=1, device_id=partner(offset), device_id_type=MESH)

    block = POINTS * FRAMES // 2
    mine = pl.ds(pl.multiple_of(core * HALF, HALF), HALF)
    other = pl.ds(pl.multiple_of((1 - core) * HALF, HALF), HALF)
    place = pl.ds(pl.multiple_of((TAPS - 1) * POINTS + core * block, POINTS), block)
    near = pltpu.make_async_copy(volt_ref.at[:, mine], frames.at[place], near_sem)
    near.start()
    blank = (TAPS - 1) * POINTS
    frames[0:blank, :] = jnp.zeros((blank, HALF), jnp.bfloat16)
    frames[blank + 2 * block :, :] = jnp.zeros((blank, HALF), jnp.bfloat16)
    for tap in range(TAPS):
        weights[tap] = jnp.broadcast_to(taps_ref[:, tap : tap + 1], (POINTS, LANES))
    added[...] = jnp.zeros(added.shape, jnp.float32)

    pl.semaphore_wait(barrier, len(ORDER))
    swap = pltpu.make_async_remote_copy(
        src_ref=volt_ref.at[:, other],
        dst_ref=frames.at[place],
        send_sem=pair_send,
        recv_sem=pair_recv,
        device_id=partner((0, 0, 0, 1)),
        device_id_type=MESH,
    )
    swap.start()
    near.wait()

    def one_frame(step, carry):
        frame = (step + (REACH - FRAMES // 2) * core) % REACH
        for part in range(POINTS // 64):
            rows = slice(part * 64, part * 64 + 64)
            total = jnp.zeros((64, HALF), jnp.float32)
            for tap in range(TAPS):
                start = pl.multiple_of((frame + tap) * POINTS + part * 64, 64)
                weight = jnp.concatenate([weights[tap, rows, :]] * GROUPS, axis=1)
                total = total + weight * frames[pl.ds(start, 64), :].astype(jnp.float32)
            filtered[rows, :] = total.astype(jnp.bfloat16)
        spectrum = jnp.dot(table_ref[...], filtered[...], preferred_element_type=jnp.float32)

        @pl.when(frame < FRAMES)
        def _():
            for group in range(GROUPS):
                main[group, pl.ds(frame, POINTS, stride=FRAMES), :] = spectrum[:, group * LANES : (group + 1) * LANES]

        @pl.when(frame >= FRAMES)
        def _():
            for group in range(GROUPS):
                tails[frame - FRAMES, pl.ds(group, POINTS, stride=GROUPS), :] = spectrum[
                    :, group * LANES : (group + 1) * LANES
                ]

        return carry

    lax.fori_loop(0, FRAMES // 2, one_frame, 0)
    swap.wait()
    lax.fori_loop(FRAMES // 2, REACH, one_frame, 0)

    def pack(target):
        for channel in range(2):
            rows = pl.ds(pl.multiple_of(target * 32 + channel * 16, 16), 16)
            for group in range(GROUPS):
                left = channel * HALF + group * LANES
                outbox[target, :, left : left + LANES] = main[group, rows, :].astype(jnp.bfloat16)
        rows = pl.ds(pl.multiple_of(target * 16, 16), 16)
        for late in range(TAPS - 1):
            left = 2 * HALF + late * LANES
            outbox[target, :, left : left + LANES] = tails[late, rows, :].astype(jnp.bfloat16)

    for offset in ORDER:
        to = partner(offset)
        target = to[0] * 16 + to[1]
        pack(target)
        pltpu.make_async_remote_copy(
            src_ref=outbox.at[target],
            dst_ref=inbox.at[me],
            send_sem=send_sem,
            recv_sem=recv_sem,
            device_id=to,
            device_id_type=MESH,
        ).start()
    pack(me)
    own = pltpu.make_async_copy(outbox.at[me], inbox.at[me], own_sem)
    own.start()
    own.wait()
    everything = inbox.at[pl.ds(0, DEVICES - 1)]
    pltpu.make_async_copy(everything, everything, recv_sem).wait()

    def merge(step, carry):
        half, first = step % 2, (step // 2) * 8
        for index in range(8):
            chip = first + index
            before = jnp.maximum(chip - 1, 0)
            for late in range(TAPS - 1):
                left = 2 * HALF + late * LANES
                tail = inbox[before * 2 + half, :, left : left + LANES].astype(jnp.float32)
                lifted[late, index * 16 : (index + 1) * 16, :] = jnp.where(chip > 0, tail, 0.0)
        for late in range(TAPS - 1):
            for group in range(GROUPS):
                added[group, pl.ds(late, 32, stride=8), :] = lifted[late, pl.ds(group, 32, stride=4), :]
        for index in range(8):
            for channel in range(2):
                for group in range(GROUPS):
                    left = channel * HALF + group * LANES
                    value = inbox[(first + index) * 2 + half, :, left : left + LANES].astype(jnp.float32)
                    extra = added[group, index * 32 + channel * 16 : index * 32 + channel * 16 + 16, :]
                    rows = pl.ds(pl.multiple_of((first + index) * 16, 16), 16)
                    lanes = pl.ds(pl.multiple_of(half * HALF + group * LANES, LANES), LANES)
                    out_ref[channel, rows, lanes] = (value + extra).astype(jnp.bfloat16)
        return carry

    lax.fori_loop(0, DEVICES // 8, merge, 0)
    pltpu.make_async_copy(everything, everything, send_sem).wait()


def correlate(x_ref, out_ref):
    step = pl.program_id(1)
    size = out_ref.shape[2]
    columns = pl.ds(pl.multiple_of(step * size, size), size)
    left = x_ref[0, :, columns]
    depth = left.shape[0]
    split = left.reshape(depth // 16, 2, 8, size)
    turned = jnp.concatenate([split[:, 1:], -split[:, :1]], axis=1).reshape(depth, size)
    dims = (((0,), (0,)), ((), ()))
    for part, operand in enumerate((left, turned)):
        result = lax.dot_general(operand, x_ref[0], dims, preferred_element_type=jnp.float32)
        out_ref[0, part] = (result * (1.0 / SPECTRA)).astype(jnp.bfloat16)


def shards(voltages, filter_taps):
    inputs = voltages.shape[1]
    vmem = pl.BlockSpec(memory_space=pltpu.VMEM)
    collected = pl.pallas_call(
        spread,
        name="spread",
        out_shape=jax.ShapeDtypeStruct((2, 2 * SPECTRA, inputs), jnp.bfloat16),
        in_specs=[pl.BlockSpec(memory_space=pl.ANY), vmem, vmem],
        out_specs=vmem,
        scratch_shapes=[
            pltpu.VMEM(((FRAMES + 2 * TAPS - 2) * POINTS, HALF), jnp.bfloat16),
            pltpu.VMEM((TAPS, POINTS, LANES), jnp.float32),
            pltpu.VMEM((POINTS, HALF), jnp.bfloat16),
            pltpu.VMEM((GROUPS, POINTS * FRAMES, LANES), jnp.float32),
            pltpu.VMEM((TAPS - 1, POINTS * GROUPS, LANES), jnp.float32),
            pltpu.VMEM((DEVICES, 16, WIDE), jnp.bfloat16),
            pltpu.VMEM((DEVICES, 16, WIDE), jnp.bfloat16),
            pltpu.VMEM((TAPS - 1, LANES, LANES), jnp.float32),
            pltpu.VMEM((GROUPS, 256, LANES), jnp.float32),
        ]
        + [pltpu.SemaphoreType.DMA(())] * 6,
        compiler_params=pltpu.CompilerParams(
            collective_id=0, has_side_effects=True, vmem_limit_bytes=58 << 20
        ),
    )(voltages, filter_taps.T, jnp.asarray(fourier_rows()))
    size = 256
    return pl.pallas_call(
        correlate,
        name="correlate",
        grid=(2, inputs // size),
        out_shape=jax.ShapeDtypeStruct((2, 2, inputs, inputs), jnp.bfloat16),
        in_specs=[pl.BlockSpec((1, 2 * SPECTRA, inputs), lambda channel, step: (channel, 0, 0))],
        out_specs=pl.BlockSpec((1, 2, size, inputs), lambda channel, step: (channel, 0, step, 0)),
        compiler_params=pltpu.CompilerParams(vmem_limit_bytes=58 << 20),
    )(collected)


def solution(mesh):
    placed = (P(("row", "col"), None), P())
    return jax.shard_map(
        shards,
        mesh=mesh,
        in_specs=placed,
        out_specs=P(("row", "col"), None, None, None),
        check_vma=False,
    )
```

time: 157 us -> 123 us (0.78)
  the two profiles are of different devices: /device:TPU:1 before, /device:TPU:35 now
where the time goes in v1:
time: 123 us; the launch traced here: 122 us
  Pallas kernels  121 us (98%)
  local copies, waits for them, and re-layouts  1.55 us (1%)
    pallas_call x1, Pallas kernels, shards(): pl.pallas_call(spread, name='spread', out_shape=jax.ShapeDtypeStruct((2,...  107 us
    pallas_call x1, Pallas kernels, shards(): pl.pallas_call(correlate, name='correlate', grid=(2, inputs // size), out...  13.8 us

profile of v1, /device:TPU:35, one launch (start us, length us, event | category | flops | bytes accessed | tf_op | source)
XLA Modules:
  0.0 122.4 jit_solution(11502613724854706783)
XLA Ops:
  0.0 1.5 %copy.4 = f32[4,512]{0,1:T(8,128)} copy(f32[4,512]{1,0:T(4,128)} %param.4) | data formatting | bytes 16384 | tf_op args[1]
  1.6 107.0 %spread.1.x_ref = bf16[2,1024,1024]{2,1,0:T(8,128)(2,1)} custom-call(bf16[2048,1024]{1,0:T(8,128)(2,1)} %volt_ref.1, f32[512,4]{1,0:T(8,128)} %bitcast.1, bf16[512,512]{1,0:T(8,128)(2,1)} %constant.2.clone.table_ref), custom_call_target="tpu_custom_call" | custom-call | tf_op jit(solution)/shard_map/spread/pallas_call | solution.py:208
  108.6 13.8 %correlate.1 = bf16[2,2,1024,1024]{3,2,1,0:T(8,128)(2,1)} custom-call(bf16[2,1024,1024]{2,1,0:T(8,128)(2,1)} %spread.1.x_ref), custom_call_target="tpu_custom_call" | custom-call | tf_op jit(solution)/shard_map/correlate/pallas_call | solution.py:231

commit v2 on v0

v2 whole, which is shorter than its diff:
```python
import itertools

import jax
import jax.numpy as jnp
import numpy as np
from jax import lax
from jax.experimental import pallas as pl
from jax.experimental.pallas import tpu as pltpu
from jax.sharding import PartitionSpec as P

MESH = pl.DeviceIdType.MESH
DEVICES = 128
POINTS = 512
TAPS = 4
SPECTRA = 512
OWN = 4
LATE = TAPS - 1
SIGNALS = 1024
HALF = SIGNALS // 2
LANES = 128
GROUPS = SIGNALS // LANES
BLOCK = 256


def orbit(offset):
    found = set()
    for turn in range(3):
        turned = offset[turn:] + offset[:turn]
        found.add(turned)
        found.add(tuple((-step) % 4 for step in turned))
    return tuple(sorted(found))


def send_order():
    hops = lambda group: sum(min(step, 4 - step) for step in group[0])
    groups = {orbit(offset) for offset in itertools.product(range(4), repeat=3)}
    ordered = []
    for group in sorted(sorted(groups), key=hops, reverse=True):
        for core in (0, 1):
            ordered += [offset + (core,) for offset in group]
    return [offset for offset in ordered if any(offset)]


ORDER = send_order()


def coordinates():
    row, col = lax.axis_index("row"), lax.axis_index("col")
    return ((col // 2) % 2) * 2 + row // 4, row % 4, col // 4, col % 2


def partner(offset):
    place = coordinates()
    x, y, z = ((own + step) % 4 for own, step in zip(place[:3], offset[:3]))
    core = (place[3] + offset[3]) % 2
    return (x % 2) * 4 + y, z * 4 + (x // 2) * 2 + core


def fourier_rows():
    turns = np.arange(POINTS // 2)[:, None] * np.arange(POINTS)[None, :] % POINTS
    phase = turns.astype(np.float32) * np.float32(2.0 * np.pi / POINTS)
    scale = np.float32(1.0) / np.sqrt(np.float32(POINTS))
    table = np.stack([np.cos(phase), -np.sin(phase)], axis=1) * scale
    table = table.reshape(DEVICES, 2, 2, POINTS).transpose(1, 0, 2, 3)
    return table.reshape(2, POINTS // 2, POINTS).astype(jnp.bfloat16)


def correlate(x_ref, y_ref, result, out_ref, sem):
    dims = (((0,), (0,)), ((), ()))
    copies = []
    for step in range(SIGNALS // BLOCK):
        first, after = step * BLOCK, (step + 1) * BLOCK
        for part, left in enumerate((x_ref, y_ref)):
            product = lax.dot_general(
                left[:, first:after], x_ref[:, first:], dims, preferred_element_type=jnp.float32
            )
            product = product * (1.0 / SPECTRA)
            result[part, first:after, first:] = product.astype(jnp.bfloat16)
            if after < SIGNALS:
                mirror = product[:, BLOCK:].T if part == 0 else -product[:, BLOCK:].T
                result[part, after:, first:after] = mirror.astype(jnp.bfloat16)
        rows = pl.ds(first, BLOCK)
        copy = pltpu.make_async_copy(result.at[:, rows], out_ref.at[:, rows], sem.at[step])
        copy.start()
        copies.append(copy)
    return copies


def spread(
    volt_ref, taps_ref, table_ref, vis_ref, x_out, y_out,
    frames, weights, filtered, main, tails, outbox, outbox_late, inbox, inbox_late, lifted, added, x_ref, y_ref, result,
    near_sem, pair_sem, send_sem, recv_sem, out_sem,
):
    row, col = lax.axis_index("row"), lax.axis_index("col")
    me = row * 16 + col
    core = col % 2
    barrier = pltpu.get_barrier_semaphore()
    for offset in ORDER:
        pl.semaphore_signal(barrier, inc=1, device_id=partner(offset), device_id_type=MESH)

    near = pltpu.make_async_copy(volt_ref, frames.at[pl.ds(LATE * POINTS, OWN * POINTS)], near_sem)
    near.start()
    for tap in range(TAPS):
        weights[tap] = jnp.broadcast_to(taps_ref[:, tap : tap + 1], (POINTS, LANES))
    added[...] = jnp.zeros(added.shape, jnp.float32)
    halo = pltpu.make_async_remote_copy(
        src_ref=volt_ref.at[pl.ds((OWN - LATE) * POINTS, LATE * POINTS)],
        dst_ref=frames.at[pl.ds(0, LATE * POINTS)],
        send_sem=pair_sem.at[0],
        recv_sem=pair_sem.at[1],
        device_id=partner((0, 0, 0, 1)),
        device_id_type=MESH,
    )

    def filter_frames(outputs, slots):
        def rows16(step, carry):
            rows = pl.ds(pl.multiple_of(step * 16, 16), 16)
            taps = [jnp.concatenate([weights[tap, rows, :]] * 2, axis=1) for tap in range(TAPS)]
            for left in range(0, SIGNALS, 256):
                lanes = slice(left, left + 256)
                values = {}
                for slot in slots:
                    at = pl.ds(pl.multiple_of(slot * POINTS + step * 16, 16), 16)
                    values[slot] = frames[at, lanes].astype(jnp.float32)
                for frame in outputs:
                    total = None
                    for tap in range(TAPS):
                        if frame + tap in values:
                            term = taps[tap] * values[frame + tap]
                            total = term if total is None else total + term
                    filtered[frame, rows, lanes] = total.astype(jnp.bfloat16)
            return carry

        lax.fori_loop(0, POINTS // 16, rows16, 0)

    def transform(channel, index, frame):
        half = index % 2
        lanes = pl.ds(pl.multiple_of(half * HALF, HALF), HALF)
        return half, jnp.dot(table_ref[channel], filtered[frame, :, lanes], preferred_element_type=jnp.float32)

    def transform_main(channel):
        def one(index, carry):
            frame = index // 2
            half, spectrum = transform(channel, index, frame)
            for group in range(GROUPS // 2):
                rows = pl.ds(frame, 2 * DEVICES, stride=OWN)
                main[half * (GROUPS // 2) + group, rows, :] = spectrum[:, group * LANES : (group + 1) * LANES]
            return carry

        lax.fori_loop(0, 2 * OWN, one, 0)

    def transform_late(channel):
        def one(index, carry):
            late = index // 2
            half, spectrum = transform(channel, index, late + OWN)
            for group in range(GROUPS // 2):
                rows = pl.ds(half * (GROUPS // 2) + group, 2 * DEVICES, stride=GROUPS)
                tails[late, rows, :] = spectrum[:, group * LANES : (group + 1) * LANES]
            return carry

        lax.fori_loop(0, 2 * LATE, one, 0)

    def pack_main(channel):
        def one(target, carry):
            rows = pl.ds(pl.multiple_of(target * 8, 8), 8)
            for group in range(GROUPS // 2):
                both = jnp.concatenate([main[group, rows, :], main[group + GROUPS // 2, rows, :]], axis=0)
                outbox[channel, target, :, group * LANES : (group + 1) * LANES] = both.astype(jnp.bfloat16)
            return carry

        lax.fori_loop(0, DEVICES, one, 0, unroll=4)

    def pack_late(channel):
        def one(target, carry):
            rows = pl.ds(pl.multiple_of(target * 16, 16), 16)
            for late in range(LATE):
                outbox_late[channel, target, :, late * LANES : (late + 1) * LANES] = tails[late, rows, :].astype(
                    jnp.bfloat16
                )
            return carry

        lax.fori_loop(0, DEVICES, one, 0, unroll=4)

    def send(channel, box, into, place, sem):
        for offset in ORDER:
            to = partner(offset)
            pltpu.make_async_remote_copy(
                src_ref=box.at[channel, to[0] * 16 + to[1]],
                dst_ref=into.at[channel, place],
                send_sem=send_sem.at[sem],
                recv_sem=recv_sem.at[sem],
                device_id=to,
                device_id_type=MESH,
            ).start()

    def send_main(channel):
        pack_main(channel)
        send(channel, outbox, inbox, me, channel)
        inbox[channel, me] = outbox[channel, me]

    def send_late(channel):
        pack_late(channel)
        send(channel, outbox_late, inbox_late, me // 2, 2 + channel)
        inbox_late[channel, me // 2] = outbox_late[channel, me]

    def arrived(channel):
        most = inbox.at[channel, pl.ds(0, DEVICES - 1)]
        pltpu.make_async_copy(most, most, recv_sem.at[channel]).wait()

        @pl.when(core == 0)
        def _():
            late = inbox_late.at[channel]
            pltpu.make_async_copy(late, late, recv_sem.at[2 + channel]).wait()

        @pl.when(core == 1)
        def _():
            late = inbox_late.at[channel, pl.ds(0, DEVICES // 2 - 1)]
            pltpu.make_async_copy(late, late, recv_sem.at[2 + channel]).wait()

    def merge(channel):
        row_of = lax.broadcasted_iota(jnp.int32, (16, LANES), 0)
        sign = jnp.where(row_of % 8 < OWN, 1.0, -1.0).astype(jnp.float32)

        def eight(step, carry):
            first = step * 8
            for index in range(8):
                chip = first + index
                before = jnp.maximum(chip - 1, 0)
                for late in range(LATE):
                    tail = inbox_late[channel, before, :, late * LANES : (late + 1) * LANES].astype(jnp.float32)
                    lifted[late, index * 16 : (index + 1) * 16, :] = jnp.where(chip > 0, tail, 0.0)
            for late in range(LATE):
                for group in range(GROUPS):
                    added[group, pl.ds(late, 16, stride=OWN), :] = lifted[late, pl.ds(group, 16, stride=GROUPS), :]
            for index in range(8):
                chip = first + index
                rows = pl.ds(pl.multiple_of(chip * 16, 16), 16)
                for group in range(GROUPS // 2):
                    lanes = slice(group * LANES, (group + 1) * LANES)
                    lower = inbox[channel, 2 * chip, :, lanes].astype(jnp.float32)
                    upper = inbox[channel, 2 * chip + 1, :, lanes].astype(jnp.float32)
                    for half in range(2):
                        whole = half * (GROUPS // 2) + group
                        extra = added[whole, index * 8 : index * 8 + 8, :]
                        part = slice(half * 8, half * 8 + 8)
                        early = lower[part] + extra
                        value = jnp.concatenate([early, upper[part]], axis=0)
                        turned = jnp.concatenate(
                            [pltpu.roll(early, OWN, 0), pltpu.roll(upper[part], OWN, 0)], axis=0
                        )
                        out = slice(whole * LANES, (whole + 1) * LANES)
                        x_ref[rows, out] = value.astype(jnp.bfloat16)
                        y_ref[rows, out] = (turned * sign).astype(jnp.bfloat16)
            return carry

        lax.fori_loop(0, DEVICES // 16, eight, 0)

    @pl.when(core == 0)
    def _():
        pl.semaphore_wait(barrier, len(ORDER))
        halo.start()
        frames[0 : LATE * POINTS, :] = jnp.zeros((LATE * POINTS, SIGNALS), jnp.bfloat16)
        near.wait()

    @pl.when(core == 1)
    def _():
        near.wait()
        filter_frames(range(OWN, OWN + LATE), range(OWN, OWN + LATE))
        transform_late(0)
        pl.semaphore_wait(barrier, len(ORDER))
        send_late(0)
        halo.wait_recv()

    filter_frames(range(OWN), range(OWN + LATE))
    transform_main(0)
    send_main(0)

    @pl.when(core == 1)
    def _():
        transform_late(1)
        send_late(1)

    transform_main(1)
    send_main(1)

    arrived(0)
    merge(0)
    copies = correlate(x_ref, y_ref, result, vis_ref, out_sem)
    arrived(1)
    merge(1)
    copies.append(pltpu.make_async_copy(x_ref, x_out, out_sem.at[4]))
    copies.append(pltpu.make_async_copy(y_ref, y_out, out_sem.at[5]))
    copies[-2].start()
    copies[-1].start()
    for channel in range(2):
        most = outbox.at[channel, pl.ds(0, DEVICES - 1)]
        pltpu.make_async_copy(most, most, send_sem.at[channel]).wait()

    @pl.when(core == 0)
    def _():
        halo.wait_send()

    @pl.when(core == 1)
    def _():
        for channel in range(2):
            most = outbox_late.at[channel, pl.ds(0, DEVICES - 1)]
            pltpu.make_async_copy(most, most, send_sem.at[2 + channel]).wait()

    for copy in copies:
        copy.wait()


def finish(vis_ref, x_in, y_in, out_ref, x_ref, y_ref, result, in_sem, out_sem):
    loads = [
        pltpu.make_async_copy(x_in, x_ref, in_sem.at[0]),
        pltpu.make_async_copy(y_in, y_ref, in_sem.at[1]),
    ]
    for load in loads:
        load.start()
    for load in loads:
        load.wait()
    done = pltpu.make_async_copy(vis_ref, out_ref.at[0], in_sem.at[2])
    done.start()
    for copy in correlate(x_ref, y_ref, result, out_ref.at[1], out_sem):
        copy.wait()
    done.wait()


def shards(voltages, filter_taps):
    inputs = voltages.shape[1]
    vmem = pl.BlockSpec(memory_space=pltpu.VMEM)
    anywhere = pl.BlockSpec(memory_space=pl.ANY)
    bf16, f32 = jnp.bfloat16, jnp.float32
    square = jax.ShapeDtypeStruct((2 * SPECTRA, inputs), bf16)
    one, x, y = pl.pallas_call(
        spread,
        name="spread",
        out_shape=[jax.ShapeDtypeStruct((2, inputs, inputs), bf16), square, square],
        in_specs=[anywhere, vmem, vmem],
        out_specs=[anywhere] * 3,
        scratch_shapes=[
            pltpu.VMEM(((OWN + LATE) * POINTS, SIGNALS), bf16),
            pltpu.VMEM((TAPS, POINTS, LANES), f32),
            pltpu.VMEM((OWN + LATE, POINTS, SIGNALS), bf16),
            pltpu.VMEM((GROUPS, DEVICES * 2 * OWN, LANES), f32),
            pltpu.VMEM((LATE, DEVICES * 2 * GROUPS, LANES), f32),
            pltpu.VMEM((2, DEVICES, 16, HALF), bf16),
            pltpu.VMEM((2, DEVICES, 16, LATE * LANES), bf16),
            pltpu.VMEM((2, DEVICES, 16, HALF), bf16),
            pltpu.VMEM((2, DEVICES // 2, 16, LATE * LANES), bf16),
            pltpu.VMEM((LATE, 128, LANES), f32),
            pltpu.VMEM((GROUPS, 64, LANES), f32),
            pltpu.VMEM((2 * SPECTRA, SIGNALS), bf16),
            pltpu.VMEM((2 * SPECTRA, SIGNALS), bf16),
            pltpu.VMEM((2, SIGNALS, SIGNALS), bf16),
            pltpu.SemaphoreType.DMA(()),
            pltpu.SemaphoreType.DMA((2,)),
            pltpu.SemaphoreType.DMA((4,)),
            pltpu.SemaphoreType.DMA((4,)),
            pltpu.SemaphoreType.DMA((6,)),
        ],
        compiler_params=pltpu.CompilerParams(
            collective_id=0, has_side_effects=True, vmem_limit_bytes=58 << 20
        ),
    )(voltages, filter_taps.T, jnp.asarray(fourier_rows()))
    return pl.pallas_call(
        finish,
        name="finish",
        out_shape=jax.ShapeDtypeStruct((2, 2, inputs, inputs), bf16),
        in_specs=[anywhere] * 3,
        out_specs=anywhere,
        scratch_shapes=[
            pltpu.VMEM((2 * SPECTRA, SIGNALS), bf16),
            pltpu.VMEM((2 * SPECTRA, SIGNALS), bf16),
            pltpu.VMEM((2, SIGNALS, SIGNALS), bf16),
            pltpu.SemaphoreType.DMA((3,)),
            pltpu.SemaphoreType.DMA((SIGNALS // BLOCK,)),
        ],
        compiler_params=pltpu.CompilerParams(vmem_limit_bytes=60 << 20),
    )(one, x, y)


def solution(mesh):
    placed = (P(("row", "col"), None), P())
    return jax.shard_map(
        shards,
        mesh=mesh,
        in_specs=placed,
        out_specs=P(("row", "col"), None, None, None),
        check_vma=False,
    )
```

time: 157 us -> 213 us (1.36)
  Pallas kernels: 0 us -> 211 us
  blocking collectives: 64.6 us -> 0 us
  waiting for transfers between devices: 32.1 us -> 0 us
  local copies, waits for them, and re-layouts: 27.6 us -> 1.55 us
  matrix products: 17.2 us -> 0 us
  other arithmetic: 8.62 us -> 0 us
  starting transfers between devices: 6.31 us -> 0 us
    pallas_call x0 -> x2, Pallas kernels: none -> 211 us  [the longest x1 130 us: shards(): pl.pallas_call(finish, name='finish', out_shape=jax.ShapeDtypeStruct((2,...]
    all_to_all x1 -> x0, blocking collectives: 64.6 us -> none  [shards(): lax.all_to_all(spectra, ('row', 'col'), split_axis=1, concat_axis=2, tile...]
    ppermute x1 -> x0, waiting for transfers between devices: 32.1 us -> none  [from_behind(): return lax.ppermute(block, axis, route)]
    dot_general x3 -> x0, matrix products: 17.2 us -> none  [the longest x1 6.58 us: shards(): jnp.einsum('jta,jtb->jab', rotated, stacked, preferred_element_type=jnp.f...]
    convert_element_type x1 -> x0, local copies, waits for them, and re-layouts: 7.76 us -> none  [shards(): return both.astype(jnp.bfloat16)]
    reshape x1 -> x0, local copies, waits for them, and re-layouts: 6.58 us -> none  [shards(): spectra = spectra.reshape(2, points // 2, local_frames, inputs)]
    ppermute x1 -> x0, starting transfers between devices: 6.31 us -> none  [from_behind(): return lax.ppermute(block, axis, route)]
    slice x4 -> x0, local copies, waits for them, and re-layouts: 6.14 us -> none  [the longest x1 2.45 us: shards(): stacked = jnp.concatenate([gathered[0], gathered[1]], axis=1)]
  transfers between devices with their start and end apart: 1 -> 0, of which waited for: 1 -> 0; matrix products, arithmetic and copies ran while one was open for 1% -> 0% of each run, Pallas kernels for 0% -> 0%
where the time goes in v2:
time: 213 us
  Pallas kernels  211 us (99%)
    pallas_call x1, Pallas kernels, shards(): pl.pallas_call(finish, name='finish', out_shape=jax.ShapeDtypeStruct((2,...  130 us
    pallas_call x1, Pallas kernels, shards(): pl.pallas_call(spread, name='spread', out_shape=[jax.ShapeDtypeStruct((2,...  80.6 us

profile of v2, /device:TPU:1, one launch (start us, length us, event | category | flops | bytes accessed | tf_op | source)
XLA Modules:
  0.0 212.6 jit_solution(15344127750053370426)
XLA Ops:
  0.0 1.5 copy.4
  1.6 80.6 %spread.1 = (bf16[2,1024,1024]{2,1,0:T(8,128)(2,1)}, bf16[1024,1024]{1,0:T(8,128)(2,1)}, bf16[1024,1024]{1,0:T(8,128)(2,1)}) custom-call(bf16[2048,1024]{1,0:T(8,128)(2,1)} %volt_ref.1, f32[512,4]{1,0:T(8,128)} %bitcast.1, bf16[2,256,512]{2,1,0:T(8,128)(2,1)} %constant.2.clone.table_ref), custom_call_target="tpu_custom_call" | custom-call | tf_op jit(solution)/shard_map/spread/pallas_call | solution.py:335
  82.2 130.4 %finish.1 = bf16[2,2,1024,1024]{3,2,1,0:T(8,128)(2,1)} custom-call(bf16[2,1024,1024]{2,1,0:T(8,128)(2,1)} %get-tuple-element.8.vis_ref, bf16[1024,1024]{1,0:T(8,128)(2,1)} %get-tuple-element.9.x_in, bf16[1024,1024]{1,0:T(8,128)(2,1)} %get-tuple-element.10.y_in), custom_call_target="tpu_custom_call" | custom-call | tf_op jit(solution)/shard_map/finish/pallas_call | solution.py:366

commit v3 on v2

--- a/solution.py
+++ b/solution.py
@@ -310,18 +310,22 @@
         copy.wait()
 
 
-def finish(vis_ref, x_in, y_in, out_ref, x_ref, y_ref, result, in_sem, out_sem):
+def finish(vis_ref, x_in, y_in, out_ref, x_ref, y_ref, through, result, in_sem, out_sem):
     loads = [
         pltpu.make_async_copy(x_in, x_ref, in_sem.at[0]),
         pltpu.make_async_copy(y_in, y_ref, in_sem.at[1]),
     ]
     for load in loads:
         load.start()
+    half = pltpu.make_async_copy(vis_ref, through, in_sem.at[2])
+    half.start()
     for load in loads:
         load.wait()
-    done = pltpu.make_async_copy(vis_ref, out_ref.at[0], in_sem.at[2])
+    copies = correlate(x_ref, y_ref, result, out_ref.at[1], out_sem)
+    half.wait()
+    done = pltpu.make_async_copy(through, out_ref.at[0], in_sem.at[3])
     done.start()
-    for copy in correlate(x_ref, y_ref, result, out_ref.at[1], out_sem):
+    for copy in copies:
         copy.wait()
     done.wait()
 
@@ -373,7 +377,8 @@
             pltpu.VMEM((2 * SPECTRA, SIGNALS), bf16),
             pltpu.VMEM((2 * SPECTRA, SIGNALS), bf16),
             pltpu.VMEM((2, SIGNALS, SIGNALS), bf16),
-            pltpu.SemaphoreType.DMA((3,)),
+            pltpu.VMEM((2, SIGNALS, SIGNALS), bf16),
+            pltpu.SemaphoreType.DMA((4,)),
             pltpu.SemaphoreType.DMA((SIGNALS // BLOCK,)),
         ],
         compiler_params=pltpu.CompilerParams(vmem_limit_bytes=60 << 20),

time: 213 us -> 90.2 us (0.42)
  Pallas kernels: 211 us -> 88.5 us
    pallas_call x1, Pallas kernels: 130 us -> 7.92 us  [shards(): pl.pallas_call(finish, name='finish', out_shape=jax.ShapeDtypeStruct((2,...]
where the time goes in v3:
time: 90.2 us; the launch traced here: 90.1 us
  Pallas kernels  88.5 us (98%)
  local copies, waits for them, and re-layouts  1.55 us (2%)
    pallas_call x1, Pallas kernels, shards(): pl.pallas_call(spread, name='spread', out_shape=[jax.ShapeDtypeStruct((2,...  80.6 us
    pallas_call x1, Pallas kernels, shards(): pl.pallas_call(finish, name='finish', out_shape=jax.ShapeDtypeStruct((2,...  7.92 us

profile of v3, /device:TPU:1, one launch (start us, length us, event | category | flops | bytes accessed | tf_op | source)
XLA Modules:
  0.0 90.1 jit_solution(13967262287679887323)
XLA Ops:
  0.0 1.5 %copy.4 = f32[4,512]{0,1:T(8,128)} copy(f32[4,512]{1,0:T(4,128)} %param.4) | data formatting | bytes 16384 | tf_op args[1]
  1.6 80.6 %spread.1 = (bf16[2,1024,1024]{2,1,0:T(8,128)(2,1)}, bf16[1024,1024]{1,0:T(8,128)(2,1)}, bf16[1024,1024]{1,0:T(8,128)(2,1)}) custom-call(bf16[2048,1024]{1,0:T(8,128)(2,1)} %volt_ref.1, f32[512,4]{1,0:T(8,128)} %bitcast.1, bf16[2,256,512]{2,1,0:T(8,128)(2,1)} %constant.2.clone.table_ref), custom_call_target="tpu_custom_call" | custom-call | tf_op jit(solution)/shard_map/spread/pallas_call | solution.py:339
  82.2 7.9 %finish.1 = bf16[2,2,1024,1024]{3,2,1,0:T(8,128)(2,1)} custom-call(bf16[2,1024,1024]{2,1,0:T(8,128)(2,1)} %get-tuple-element.8.vis_ref, bf16[1024,1024]{1,0:T(8,128)(2,1)} %get-tuple-element.9.x_in, bf16[1024,1024]{1,0:T(8,128)(2,1)} %get-tuple-element.10.y_in), custom_call_target="tpu_custom_call" | custom-call | tf_op jit(solution)/shard_map/finish/pallas_call | solution.py:370

commit v4 on v2

--- a/solution.py
+++ b/solution.py
@@ -65,7 +65,7 @@
     return table.reshape(2, POINTS // 2, POINTS).astype(jnp.bfloat16)
 
 
-def correlate(x_ref, y_ref, result, out_ref, sem):
+def correlate(x_ref, y_ref, result, out_ref=None, sem=None):
     dims = (((0,), (0,)), ((), ()))
     copies = []
     for step in range(SIGNALS // BLOCK):
@@ -74,11 +74,13 @@
             product = lax.dot_general(
                 left[:, first:after], x_ref[:, first:], dims, preferred_element_type=jnp.float32
             )
-            product = product * (1.0 / SPECTRA)
-            result[part, first:after, first:] = product.astype(jnp.bfloat16)
+            product = (product * (1.0 / SPECTRA)).astype(jnp.bfloat16)
+            result[part, first:after, first:] = product
             if after < SIGNALS:
-                mirror = product[:, BLOCK:].T if part == 0 else -product[:, BLOCK:].T
-                result[part, after:, first:after] = mirror.astype(jnp.bfloat16)
+                mirror = product[:, BLOCK:].T
+                result[part, after:, first:after] = mirror if part == 0 else -mirror
+        if out_ref is None:
+            continue
         rows = pl.ds(first, BLOCK)
         copy = pltpu.make_async_copy(result.at[:, rows], out_ref.at[:, rows], sem.at[step])
         copy.start()
@@ -87,9 +89,9 @@
 
 
 def spread(
-    volt_ref, taps_ref, table_ref, vis_ref, x_out, y_out,
-    frames, weights, filtered, main, tails, outbox, outbox_late, inbox, inbox_late, lifted, added, x_ref, y_ref, result,
-    near_sem, pair_sem, send_sem, recv_sem, out_sem,
+    volt_ref, taps_ref, table_ref, result, x_ref, y_ref,
+    frames, weights, filtered, main, tails, outbox, outbox_late, inbox, inbox_late, lifted, added,
+    near_sem, pair_sem, send_sem, recv_sem,
 ):
     row, col = lax.axis_index("row"), lax.axis_index("col")
     me = row * 16 + col
@@ -100,8 +102,11 @@
 
     near = pltpu.make_async_copy(volt_ref, frames.at[pl.ds(LATE * POINTS, OWN * POINTS)], near_sem)
     near.start()
-    for tap in range(TAPS):
-        weights[tap] = jnp.broadcast_to(taps_ref[:, tap : tap + 1], (POINTS, LANES))
+    padded = jnp.concatenate([taps_ref[...], jnp.zeros((LANES - TAPS, POINTS), jnp.float32)], axis=0)
+    for first in range(0, POINTS, LANES):
+        columns = padded[:, first : first + LANES].T
+        for tap in range(TAPS):
+            weights[tap, first : first + LANES, :] = jnp.broadcast_to(columns[:, tap : tap + 1], (LANES, LANES))
     added[...] = jnp.zeros(added.shape, jnp.float32)
     halo = pltpu.make_async_remote_copy(
         src_ref=volt_ref.at[pl.ds((OWN - LATE) * POINTS, LATE * POINTS)],
@@ -192,16 +197,6 @@
                 device_id=to,
                 device_id_type=MESH,
             ).start()
-
-    def send_main(channel):
-        pack_main(channel)
-        send(channel, outbox, inbox, me, channel)
-        inbox[channel, me] = outbox[channel, me]
-
-    def send_late(channel):
-        pack_late(channel)
-        send(channel, outbox_late, inbox_late, me // 2, 2 + channel)
-        inbox_late[channel, me // 2] = outbox_late[channel, me]
 
     def arrived(channel):
         most = inbox.at[channel, pl.ds(0, DEVICES - 1)]
@@ -255,43 +250,47 @@
 
         lax.fori_loop(0, DEVICES // 16, eight, 0)
 
+    near.wait()
+
     @pl.when(core == 0)
     def _():
+        frames[0 : LATE * POINTS, :] = jnp.zeros((LATE * POINTS, SIGNALS), jnp.bfloat16)
+        filter_frames(range(OWN), range(OWN + LATE))
+        transform_main(0)
+        pack_main(0)
         pl.semaphore_wait(barrier, len(ORDER))
         halo.start()
-        frames[0 : LATE * POINTS, :] = jnp.zeros((LATE * POINTS, SIGNALS), jnp.bfloat16)
-        near.wait()
+        send(0, outbox, inbox, me, 0)
 
     @pl.when(core == 1)
     def _():
-        near.wait()
         filter_frames(range(OWN, OWN + LATE), range(OWN, OWN + LATE))
         transform_late(0)
+        pack_late(0)
         pl.semaphore_wait(barrier, len(ORDER))
-        send_late(0)
+        send(0, outbox_late, inbox_late, me // 2, 2)
+        inbox_late[0, me // 2] = outbox_late[0, me]
         halo.wait_recv()
-
-    filter_frames(range(OWN), range(OWN + LATE))
-    transform_main(0)
-    send_main(0)
-
-    @pl.when(core == 1)
-    def _():
+        filter_frames(range(OWN), range(OWN + LATE))
+        transform_main(0)
+        pack_main(0)
+        send(0, outbox, inbox, me, 0)
         transform_late(1)
-        send_late(1)
-
+        pack_late(1)
+        send(1, outbox_late, inbox_late, me // 2, 3)
+        inbox_late[1, me // 2] = outbox_late[1, me]
+
+    inbox[0, me] = outbox[0, me]
     transform_main(1)
-    send_main(1)
+    pack_main(1)
+    send(1, outbox, inbox, me, 1)
+    inbox[1, me] = outbox[1, me]
 
     arrived(0)
     merge(0)
-    copies = correlate(x_ref, y_ref, result, vis_ref, out_sem)
+    correlate(x_ref, y_ref, result)
     arrived(1)
     merge(1)
-    copies.append(pltpu.make_async_copy(x_ref, x_out, out_sem.at[4]))
-    copies.append(pltpu.make_async_copy(y_ref, y_out, out_sem.at[5]))
-    copies[-2].start()
-    copies[-1].start()
     for channel in range(2):
         most = outbox.at[channel, pl.ds(0, DEVICES - 1)]
         pltpu.make_async_copy(most, most, send_sem.at[channel]).wait()
@@ -306,20 +305,9 @@
             most = outbox_late.at[channel, pl.ds(0, DEVICES - 1)]
             pltpu.make_async_copy(most, most, send_sem.at[2 + channel]).wait()
 
-    for copy in copies:
-        copy.wait()
-
-
-def finish(vis_ref, x_in, y_in, out_ref, x_ref, y_ref, result, in_sem, out_sem):
-    loads = [
-        pltpu.make_async_copy(x_in, x_ref, in_sem.at[0]),
-        pltpu.make_async_copy(y_in, y_ref, in_sem.at[1]),
-    ]
-    for load in loads:
-        load.start()
-    for load in loads:
-        load.wait()
-    done = pltpu.make_async_copy(vis_ref, out_ref.at[0], in_sem.at[2])
+
+def finish(vis_ref, x_ref, y_ref, out_ref, result, done_sem, out_sem):
+    done = pltpu.make_async_copy(vis_ref, out_ref.at[0], done_sem)
     done.start()
     for copy in correlate(x_ref, y_ref, result, out_ref.at[1], out_sem):
         copy.wait()
@@ -331,13 +319,14 @@
     vmem = pl.BlockSpec(memory_space=pltpu.VMEM)
     anywhere = pl.BlockSpec(memory_space=pl.ANY)
     bf16, f32 = jnp.bfloat16, jnp.float32
-    square = jax.ShapeDtypeStruct((2 * SPECTRA, inputs), bf16)
-    one, x, y = pl.pallas_call(
+    square = pltpu.VMEM((2 * SPECTRA, inputs), bf16)
+    kept = [pltpu.VMEM((2, inputs, inputs), bf16), square, square]
+    kept = pl.pallas_call(
         spread,
         name="spread",
-        out_shape=[jax.ShapeDtypeStruct((2, inputs, inputs), bf16), square, square],
+        out_shape=kept,
         in_specs=[anywhere, vmem, vmem],
-        out_specs=[anywhere] * 3,
+        out_specs=[vmem] * 3,
         scratch_shapes=[
             pltpu.VMEM(((OWN + LATE) * POINTS, SIGNALS), bf16),
             pltpu.VMEM((TAPS, POINTS, LANES), f32),
@@ -350,34 +339,29 @@
             pltpu.VMEM((2, DEVICES // 2, 16, LATE * LANES), bf16),
             pltpu.VMEM((LATE, 128, LANES), f32),
             pltpu.VMEM((GROUPS, 64, LANES), f32),
-            pltpu.VMEM((2 * SPECTRA, SIGNALS), bf16),
-            pltpu.VMEM((2 * SPECTRA, SIGNALS), bf16),
-            pltpu.VMEM((2, SIGNALS, SIGNALS), bf16),
             pltpu.SemaphoreType.DMA(()),
             pltpu.SemaphoreType.DMA((2,)),
             pltpu.SemaphoreType.DMA((4,)),
             pltpu.SemaphoreType.DMA((4,)),
-            pltpu.SemaphoreType.DMA((6,)),
         ],
         compiler_params=pltpu.CompilerParams(
-            collective_id=0, has_side_effects=True, vmem_limit_bytes=58 << 20
+            collective_id=0, has_side_effects=True, vmem_limit_bytes=50 << 20
         ),
-    )(voltages, filter_taps.T, jnp.asarray(fourier_rows()))
+    )(voltages, filter_taps, jnp.asarray(fourier_rows()))
+    kept = [pltpu.with_memory_space_constraint(array, pltpu.VMEM) for array in kept]
     return pl.pallas_call(
         finish,
         name="finish",
         out_shape=jax.ShapeDtypeStruct((2, 2, inputs, inputs), bf16),
-        in_specs=[anywhere] * 3,
+        in_specs=[vmem] * 3,
         out_specs=anywhere,
         scratch_shapes=[
-            pltpu.VMEM((2 * SPECTRA, SIGNALS), bf16),
-            pltpu.VMEM((2 * SPECTRA, SIGNALS), bf16),
             pltpu.VMEM((2, SIGNALS, SIGNALS), bf16),
-            pltpu.SemaphoreType.DMA((3,)),
+            pltpu.SemaphoreType.DMA(()),
             pltpu.SemaphoreType.DMA((SIGNALS // BLOCK,)),
         ],
-        compiler_params=pltpu.CompilerParams(vmem_limit_bytes=60 << 20),
-    )(one, x, y)
+        compiler_params=pltpu.CompilerParams(vmem_limit_bytes=48 << 20),
+    )(*kept)
 
 
 def solution(mesh):

time: 213 us -> 82.8 us (0.39)
  Pallas kernels: 211 us -> 82.7 us
    pallas_call x1, Pallas kernels: 130 us -> 4.17 us  [shards(): pl.pallas_call(finish, name='finish', out_shape=jax.ShapeDtypeStruct((2,...]
where the time goes in v4:
time: 82.8 us; the launch traced here: 82.7 us
  Pallas kernels  82.7 us (100%)
    pallas_call x1, Pallas kernels, shards(): pl.pallas_call(spread, name='spread', out_shape=kept, in_specs=[anywhere,...  78.5 us
    pallas_call x1, Pallas kernels, shards(): pl.pallas_call(finish, name='finish', out_shape=jax.ShapeDtypeStruct((2,...  4.17 us

profile of v4, /device:TPU:1, one launch (start us, length us, event | category | flops | bytes accessed | tf_op | source)
XLA Modules:
  0.0 82.7 jit_solution(7259771573968359618)
XLA Ops:
  0.0 78.5 %spread.1 = (bf16[2,1024,1024]{2,1,0:T(8,128)(2,1)S(1)}, bf16[1024,1024]{1,0:T(8,128)(2,1)S(1)}, bf16[1024,1024]{1,0:T(8,128)(2,1)S(1)}) custom-call(bf16[2048,1024]{1,0:T(8,128)(2,1)} %volt_ref.1, f32[4,512]{1,0:T(4,128)} %taps_ref.1, bf16[2,256,512]{2,1,0:T(8,128)(2,1)} %constant.2.clone.table_ref), custom_call_target="tpu_custom_call" | custom-call | tf_op jit(solution)/shard_map/spread/pallas_call | solution.py:324
  78.5 4.2 %finish.1 = bf16[2,2,1024,1024]{3,2,1,0:T(8,128)(2,1)} custom-call(bf16[2,1024,1024]{2,1,0:T(8,128)(2,1)S(1)} %get-tuple-element.8.vis_ref, bf16[1024,1024]{1,0:T(8,128)(2,1)S(1)} %get-tuple-element.9.x_ref, bf16[1024,1024]{1,0:T(8,128)(2,1)S(1)} %get-tuple-element.10.y_ref), custom_call_target="tpu_custom_call" | custom-call | tf_op jit(solution)/shard_map/finish/pallas_call | solution.py:352

commit v5 on v4

--- a/solution.py
+++ b/solution.py
@@ -20,6 +20,7 @@
 LANES = 128
 GROUPS = SIGNALS // LANES
 BLOCK = 256
+STARTS = (0, 1024, 1792, 2304, 2560)
 
 
 def orbit(offset):
@@ -42,6 +43,8 @@
 
 
 ORDER = send_order()
+ODD = [offset for offset in ORDER if offset[1] % 2 == 1]
+EVEN = [offset for offset in ORDER if offset[1] % 2 == 0]
 
 
 def coordinates():
@@ -65,15 +68,14 @@
     return table.reshape(2, POINTS // 2, POINTS).astype(jnp.bfloat16)
 
 
-def correlate(x_ref, y_ref, result, out_ref=None, sem=None):
-    dims = (((0,), (0,)), ((), ()))
+def correlate(x_ref, y_ref, depth, result, base=None, out_ref=None, sem=None):
     copies = []
     for step in range(SIGNALS // BLOCK):
         first, after = step * BLOCK, (step + 1) * BLOCK
-        for part, left in enumerate((x_ref, y_ref)):
-            product = lax.dot_general(
-                left[:, first:after], x_ref[:, first:], dims, preferred_element_type=jnp.float32
-            )
+        for part in range(2):
+            product = block_row(x_ref, y_ref, depth, step, part)
+            if base is not None:
+                product = product + base[part, :, STARTS[step] : STARTS[step + 1]]
             product = (product * (1.0 / SPECTRA)).astype(jnp.bfloat16)
             result[part, first:after, first:] = product
             if after < SIGNALS:
@@ -88,9 +90,19 @@
     return copies
 
 
+def block_row(x_ref, y_ref, depth, step, part):
+    left = y_ref if part else x_ref
+    return lax.dot_general(
+        left[0:depth, step * BLOCK : (step + 1) * BLOCK],
+        x_ref[0:depth, step * BLOCK :],
+        (((0,), (0,)), ((), ())),
+        preferred_element_type=jnp.float32,
+    )
+
+
 def spread(
-    volt_ref, taps_ref, table_ref, result, x_ref, y_ref,
-    frames, weights, filtered, main, tails, outbox, outbox_late, inbox, inbox_late, lifted, added,
+    volt_ref, taps_ref, table_ref, result, sums, x_last, y_last,
+    frames, weights, filtered, main, tails, outbox, outbox_late, inbox, inbox_late, lifted, added, x_ref, y_ref,
     near_sem, pair_sem, send_sem, recv_sem,
 ):
     row, col = lax.axis_index("row"), lax.axis_index("col")
@@ -186,8 +198,8 @@
 
         lax.fori_loop(0, DEVICES, one, 0, unroll=4)
 
-    def send(channel, box, into, place, sem):
-        for offset in ORDER:
+    def send(channel, box, into, place, sem, order=ORDER):
+        for offset in order:
             to = partner(offset)
             pltpu.make_async_remote_copy(
                 src_ref=box.at[channel, to[0] * 16 + to[1]],
@@ -198,10 +210,11 @@
                 device_id_type=MESH,
             ).start()
 
-    def arrived(channel):
-        most = inbox.at[channel, pl.ds(0, DEVICES - 1)]
-        pltpu.make_async_copy(most, most, recv_sem.at[channel]).wait()
-
+    def arrived(channel, count, sem):
+        most = inbox.at[channel, pl.ds(0, count)]
+        pltpu.make_async_copy(most, most, recv_sem.at[sem]).wait()
+
+    def arrived_late(channel):
         @pl.when(core == 0)
         def _():
             late = inbox_late.at[channel]
@@ -212,12 +225,12 @@
             late = inbox_late.at[channel, pl.ds(0, DEVICES // 2 - 1)]
             pltpu.make_async_copy(late, late, recv_sem.at[2 + channel]).wait()
 
-    def merge(channel):
+    def merge(channel, count, chunk, x_to, y_to):
         row_of = lax.broadcasted_iota(jnp.int32, (16, LANES), 0)
         sign = jnp.where(row_of % 8 < OWN, 1.0, -1.0).astype(jnp.float32)
 
         def eight(step, carry):
-            first = step * 8
+            first = chunk(step) * 8
             for index in range(8):
                 chip = first + index
                 before = jnp.maximum(chip - 1, 0)
@@ -229,7 +242,7 @@
                     added[group, pl.ds(late, 16, stride=OWN), :] = lifted[late, pl.ds(group, 16, stride=GROUPS), :]
             for index in range(8):
                 chip = first + index
-                rows = pl.ds(pl.multiple_of(chip * 16, 16), 16)
+                rows = pl.ds(pl.multiple_of((step * 8 + index) * 16, 16), 16)
                 for group in range(GROUPS // 2):
                     lanes = slice(group * LANES, (group + 1) * LANES)
                     lower = inbox[channel, 2 * chip, :, lanes].astype(jnp.float32)
@@ -244,11 +257,11 @@
                             [pltpu.roll(early, OWN, 0), pltpu.roll(upper[part], OWN, 0)], axis=0
                         )
                         out = slice(whole * LANES, (whole + 1) * LANES)
-                        x_ref[rows, out] = value.astype(jnp.bfloat16)
-                        y_ref[rows, out] = (turned * sign).astype(jnp.bfloat16)
-            return carry
-
-        lax.fori_loop(0, DEVICES // 16, eight, 0)
+                        x_to[rows, out] = value.astype(jnp.bfloat16)
+                        y_to[rows, out] = (turned * sign).astype(jnp.bfloat16)
+            return carry
+
+        lax.fori_loop(0, count, eight, 0)
 
     near.wait()
 
@@ -283,17 +296,26 @@
     inbox[0, me] = outbox[0, me]
     transform_main(1)
     pack_main(1)
-    send(1, outbox, inbox, me, 1)
+    send(1, outbox, inbox, me, 1, ODD)
+    send(1, outbox, inbox, me, 4, EVEN)
     inbox[1, me] = outbox[1, me]
 
-    arrived(0)
-    merge(0)
-    correlate(x_ref, y_ref, result)
-    arrived(1)
-    merge(1)
-    for channel in range(2):
-        most = outbox.at[channel, pl.ds(0, DEVICES - 1)]
-        pltpu.make_async_copy(most, most, send_sem.at[channel]).wait()
+    y = row % 4
+    arrived(0, DEVICES - 1, 0)
+    arrived_late(0)
+    merge(0, 8, lambda step: step, x_ref, y_ref)
+    correlate(x_ref, y_ref, 2 * SPECTRA, result)
+    arrived_late(1)
+    arrived(1, len(ODD), 1)
+    merge(1, 4, lambda step: step // 2 * 4 + (y + 1 + step % 2 * 2) % 4, x_ref, y_ref)
+    for step in range(SIGNALS // BLOCK):
+        for part in range(2):
+            sums[part, :, STARTS[step] : STARTS[step + 1]] = block_row(x_ref, y_ref, SPECTRA, step, part)
+    arrived(1, len(EVEN), 4)
+    merge(1, 4, lambda step: step // 2 * 4 + (y + step % 2 * 2) % 4, x_last, y_last)
+    for channel, count, sem in ((0, DEVICES - 1, 0), (1, len(ODD), 1), (1, len(EVEN), 4)):
+        most = outbox.at[channel, pl.ds(0, count)]
+        pltpu.make_async_copy(most, most, send_sem.at[sem]).wait()
 
     @pl.when(core == 0)
     def _():
@@ -306,10 +328,10 @@
             pltpu.make_async_copy(most, most, send_sem.at[2 + channel]).wait()
 
 
-def finish(vis_ref, x_ref, y_ref, out_ref, result, done_sem, out_sem):
+def finish(vis_ref, sums, x_ref, y_ref, out_ref, result, done_sem, out_sem):
     done = pltpu.make_async_copy(vis_ref, out_ref.at[0], done_sem)
     done.start()
-    for copy in correlate(x_ref, y_ref, result, out_ref.at[1], out_sem):
+    for copy in correlate(x_ref, y_ref, SPECTRA, result, sums, out_ref.at[1], out_sem):
         copy.wait()
     done.wait()
 
@@ -319,14 +341,14 @@
     vmem = pl.BlockSpec(memory_space=pltpu.VMEM)
     anywhere = pl.BlockSpec(memory_space=pl.ANY)
     bf16, f32 = jnp.bfloat16, jnp.float32
-    square = pltpu.VMEM((2 * SPECTRA, inputs), bf16)
-    kept = [pltpu.VMEM((2, inputs, inputs), bf16), square, square]
+    last = pltpu.VMEM((SPECTRA, inputs), bf16)
+    kept = [pltpu.VMEM((2, inputs, inputs), bf16), pltpu.VMEM((2, BLOCK, STARTS[-1]), f32), last, last]
     kept = pl.pallas_call(
         spread,
         name="spread",
         out_shape=kept,
         in_specs=[anywhere, vmem, vmem],
-        out_specs=[vmem] * 3,
+        out_specs=[vmem] * 4,
         scratch_shapes=[
             pltpu.VMEM(((OWN + LATE) * POINTS, SIGNALS), bf16),
             pltpu.VMEM((TAPS, POINTS, LANES), f32),
@@ -339,13 +361,15 @@
             pltpu.VMEM((2, DEVICES // 2, 16, LATE * LANES), bf16),
             pltpu.VMEM((LATE, 128, LANES), f32),
             pltpu.VMEM((GROUPS, 64, LANES), f32),
+            pltpu.VMEM((2 * SPECTRA, SIGNALS), bf16),
+            pltpu.VMEM((2 * SPECTRA, SIGNALS), bf16),
             pltpu.SemaphoreType.DMA(()),
             pltpu.SemaphoreType.DMA((2,)),
-            pltpu.SemaphoreType.DMA((4,)),
-            pltpu.SemaphoreType.DMA((4,)),
+            pltpu.SemaphoreType.DMA((5,)),
+            pltpu.SemaphoreType.DMA((5,)),
         ],
         compiler_params=pltpu.CompilerParams(
-            collective_id=0, has_side_effects=True, vmem_limit_bytes=50 << 20
+            collective_id=0, has_side_effects=True, vmem_limit_bytes=48 << 20
         ),
     )(voltages, filter_taps, jnp.asarray(fourier_rows()))
     kept = [pltpu.with_memory_space_constraint(array, pltpu.VMEM) for array in kept]
@@ -353,7 +377,7 @@
         finish,
         name="finish",
         out_shape=jax.ShapeDtypeStruct((2, 2, inputs, inputs), bf16),
-        in_specs=[vmem] * 3,
+        in_specs=[vmem] * 4,
         out_specs=anywhere,
         scratch_shapes=[
             pltpu.VMEM((2, SIGNALS, SIGNALS), bf16),

time: 82.8 us -> 83.1 us (level); the launches traced: 82.7 us -> 81.5 us
  Pallas kernels: 82.7 us -> 81.3 us
where the time goes in v5:
time: 83.1 us; the launch traced here: 81.5 us
  Pallas kernels  81.3 us (98%)
    pallas_call x1, Pallas kernels, shards(): pl.pallas_call(spread, name='spread', out_shape=kept, in_specs=[anywhere,...  78 us
    pallas_call x1, Pallas kernels, shards(): pl.pallas_call(finish, name='finish', out_shape=jax.ShapeDtypeStruct((2,...  3.34 us

profile of v5, /device:TPU:1, one launch (start us, length us, event | category | flops | bytes accessed | tf_op | source)
XLA Modules:
  0.0 81.5 jit_solution(17952336613594366680)
XLA Ops:
  0.0 78.0 %spread.1 = (bf16[2,1024,1024]{2,1,0:T(8,128)(2,1)S(1)}, f32[2,256,2560]{2,1,0:T(8,128)S(1)}, bf16[512,1024]{1,0:T(8,128)(2,1)S(1)}, bf16[512,1024]{1,0:T(8,128)(2,1)S(1)}) custom-call(bf16[2048,1024]{1,0:T(8,128)(2,1)} %volt_ref.1, f32[4,512]{1,0:T(4,128)} %taps_ref.1, bf16[2,256,512]{2,1,0:T(8,128)(2,1)} %constant.2.clone.table_ref), custom_call_target="tpu_custom_call" | custom-call | tf_op jit(solution)/shard_map/spread/pallas_call | solution.py:346
  78.0 3.3 %finish.1 = bf16[2,2,1024,1024]{3,2,1,0:T(8,128)(2,1)} custom-call(bf16[2,1024,1024]{2,1,0:T(8,128)(2,1)S(1)} %get-tuple-element.9.vis_ref, f32[2,256,2560]{2,1,0:T(8,128)S(1)} %get-tuple-element.10.sums, bf16[512,1024]{1,0:T(8,128)(2,1)S(1)} %get-tuple-element.11.x_ref, bf16[512,1024]{1,0:T(8,128)(2,1)S(1)} %get-tuple-element.12.y_ref), custom_call_target="tpu_custom_call" | custom-call | tf_op jit(solution)/shard_map/finish/pallas_call | solution.py:376

commit v6 on v5

--- a/solution.py
+++ b/solution.py
@@ -43,8 +43,12 @@
 
 
 ORDER = send_order()
-ODD = [offset for offset in ORDER if offset[1] % 2 == 1]
-EVEN = [offset for offset in ORDER if offset[1] % 2 == 0]
+CHIPS = list(dict.fromkeys(offset[:3] for offset in ORDER))
+EDGES = (0, 22, 51, 64)
+LOTS = [CHIPS[first:last] for first, last in zip(EDGES, EDGES[1:])]
+SENDS = [[offset for offset in ORDER if offset[:3] in lot] for lot in LOTS]
+LOT_SEM = (1, 4, 5)
+LAST = 16 * len(LOTS[-1])
 
 
 def coordinates():
@@ -225,43 +229,53 @@
             late = inbox_late.at[channel, pl.ds(0, DEVICES // 2 - 1)]
             pltpu.make_async_copy(late, late, recv_sem.at[2 + channel]).wait()
 
-    def merge(channel, count, chunk, x_to, y_to):
-        row_of = lax.broadcasted_iota(jnp.int32, (16, LANES), 0)
-        sign = jnp.where(row_of % 8 < OWN, 1.0, -1.0).astype(jnp.float32)
-
+    def lift(channel):
         def eight(step, carry):
-            first = chunk(step) * 8
             for index in range(8):
-                chip = first + index
+                chip = step * 8 + index
                 before = jnp.maximum(chip - 1, 0)
                 for late in range(LATE):
                     tail = inbox_late[channel, before, :, late * LANES : (late + 1) * LANES].astype(jnp.float32)
                     lifted[late, index * 16 : (index + 1) * 16, :] = jnp.where(chip > 0, tail, 0.0)
             for late in range(LATE):
                 for group in range(GROUPS):
-                    added[group, pl.ds(late, 16, stride=OWN), :] = lifted[late, pl.ds(group, 16, stride=GROUPS), :]
+                    rows = pl.ds(step * 64 + late, 16, stride=OWN)
+                    added[group, rows, :] = lifted[late, pl.ds(group, 16, stride=GROUPS), :]
+            return carry
+
+        lax.fori_loop(0, DEVICES // 16, eight, 0)
+
+    def merge(channel, chip, rows, x_to, y_to):
+        row_of = lax.broadcasted_iota(jnp.int32, (16, LANES), 0)
+        sign = jnp.where(row_of % 8 < OWN, 1.0, -1.0).astype(jnp.float32)
+        extra_rows = pl.ds(pl.multiple_of(chip * 8, 8), 8)
+        for group in range(GROUPS // 2):
+            lanes = slice(group * LANES, (group + 1) * LANES)
+            lower = inbox[channel, 2 * chip, :, lanes].astype(jnp.float32)
+            upper = inbox[channel, 2 * chip + 1, :, lanes].astype(jnp.float32)
+            for half in range(2):
+                whole = half * (GROUPS // 2) + group
+                part = slice(half * 8, half * 8 + 8)
+                early = lower[part] + added[whole, extra_rows, :]
+                value = jnp.concatenate([early, upper[part]], axis=0)
+                turned = jnp.concatenate([pltpu.roll(early, OWN, 0), pltpu.roll(upper[part], OWN, 0)], axis=0)
+                out = slice(whole * LANES, (whole + 1) * LANES)
+                x_to[rows, out] = value.astype(jnp.bfloat16)
+                y_to[rows, out] = (turned * sign).astype(jnp.bfloat16)
+
+    def merge_whole(channel):
+        def eight(step, carry):
             for index in range(8):
-                chip = first + index
-                rows = pl.ds(pl.multiple_of((step * 8 + index) * 16, 16), 16)
-                for group in range(GROUPS // 2):
-                    lanes = slice(group * LANES, (group + 1) * LANES)
-                    lower = inbox[channel, 2 * chip, :, lanes].astype(jnp.float32)
-                    upper = inbox[channel, 2 * chip + 1, :, lanes].astype(jnp.float32)
-                    for half in range(2):
-                        whole = half * (GROUPS // 2) + group
-                        extra = added[whole, index * 8 : index * 8 + 8, :]
-                        part = slice(half * 8, half * 8 + 8)
-                        early = lower[part] + extra
-                        value = jnp.concatenate([early, upper[part]], axis=0)
-                        turned = jnp.concatenate(
-                            [pltpu.roll(early, OWN, 0), pltpu.roll(upper[part], OWN, 0)], axis=0
-                        )
-                        out = slice(whole * LANES, (whole + 1) * LANES)
-                        x_to[rows, out] = value.astype(jnp.bfloat16)
-                        y_to[rows, out] = (turned * sign).astype(jnp.bfloat16)
-            return carry
-
-        lax.fori_loop(0, count, eight, 0)
+                chip = step * 8 + index
+                merge(channel, chip, pl.ds(pl.multiple_of(chip * 16, 16), 16), x_ref, y_ref)
+            return carry
+
+        lax.fori_loop(0, DEVICES // 16, eight, 0)
+
+    def merge_lot(channel, lot, x_to, y_to):
+        for index, offset in enumerate(LOTS[lot]):
+            place = partner(offset + (0,))
+            merge(channel, place[0] * 8 + place[1] // 2, slice(index * 16, index * 16 + 16), x_to, y_to)
 
     near.wait()
 
@@ -296,24 +310,28 @@
     inbox[0, me] = outbox[0, me]
     transform_main(1)
     pack_main(1)
-    send(1, outbox, inbox, me, 1, ODD)
-    send(1, outbox, inbox, me, 4, EVEN)
+    for sends, sem in zip(SENDS, LOT_SEM):
+        send(1, outbox, inbox, me, sem, sends)
     inbox[1, me] = outbox[1, me]
 
-    y = row % 4
     arrived(0, DEVICES - 1, 0)
     arrived_late(0)
-    merge(0, 8, lambda step: step, x_ref, y_ref)
+    lift(0)
+    merge_whole(0)
     correlate(x_ref, y_ref, 2 * SPECTRA, result)
     arrived_late(1)
-    arrived(1, len(ODD), 1)
-    merge(1, 4, lambda step: step // 2 * 4 + (y + 1 + step % 2 * 2) % 4, x_ref, y_ref)
-    for step in range(SIGNALS // BLOCK):
-        for part in range(2):
-            sums[part, :, STARTS[step] : STARTS[step + 1]] = block_row(x_ref, y_ref, SPECTRA, step, part)
-    arrived(1, len(EVEN), 4)
-    merge(1, 4, lambda step: step // 2 * 4 + (y + step % 2 * 2) % 4, x_last, y_last)
-    for channel, count, sem in ((0, DEVICES - 1, 0), (1, len(ODD), 1), (1, len(EVEN), 4)):
+    lift(1)
+    for lot in range(len(LOTS) - 1):
+        arrived(1, len(SENDS[lot]), LOT_SEM[lot])
+        merge_lot(1, lot, x_ref, y_ref)
+        for step in range(SIGNALS // BLOCK):
+            columns = slice(STARTS[step], STARTS[step + 1])
+            for part in range(2):
+                product = block_row(x_ref, y_ref, 16 * len(LOTS[lot]), step, part)
+                sums[part, :, columns] = product if lot == 0 else sums[part, :, columns] + product
+    arrived(1, len(SENDS[-1]), LOT_SEM[-1])
+    merge_lot(1, len(LOTS) - 1, x_last, y_last)
+    for channel, count, sem in [(0, DEVICES - 1, 0)] + [(1, len(sends), sem) for sends, sem in zip(SENDS, LOT_SEM)]:
         most = outbox.at[channel, pl.ds(0, count)]
         pltpu.make_async_copy(most, most, send_sem.at[sem]).wait()
 
@@ -331,7 +349,7 @@
 def finish(vis_ref, sums, x_ref, y_ref, out_ref, result, done_sem, out_sem):
     done = pltpu.make_async_copy(vis_ref, out_ref.at[0], done_sem)
     done.start()
-    for copy in correlate(x_ref, y_ref, SPECTRA, result, sums, out_ref.at[1], out_sem):
+    for copy in correlate(x_ref, y_ref, LAST, result, sums, out_ref.at[1], out_sem):
         copy.wait()
     done.wait()
 
@@ -341,7 +359,7 @@
     vmem = pl.BlockSpec(memory_space=pltpu.VMEM)
     anywhere = pl.BlockSpec(memory_space=pl.ANY)
     bf16, f32 = jnp.bfloat16, jnp.float32
-    last = pltpu.VMEM((SPECTRA, inputs), bf16)
+    last = pltpu.VMEM((LAST, inputs), bf16)
     kept = [pltpu.VMEM((2, inputs, inputs), bf16), pltpu.VMEM((2, BLOCK, STARTS[-1]), f32), last, last]
     kept = pl.pallas_call(
         spread,
@@ -360,13 +378,13 @@
             pltpu.VMEM((2, DEVICES, 16, HALF), bf16),
             pltpu.VMEM((2, DEVICES // 2, 16, LATE * LANES), bf16),
             pltpu.VMEM((LATE, 128, LANES), f32),
-            pltpu.VMEM((GROUPS, 64, LANES), f32),
+            pltpu.VMEM((GROUPS, 4 * DEVICES, LANES), f32),
             pltpu.VMEM((2 * SPECTRA, SIGNALS), bf16),
             pltpu.VMEM((2 * SPECTRA, SIGNALS), bf16),
             pltpu.SemaphoreType.DMA(()),
             pltpu.SemaphoreType.DMA((2,)),
-            pltpu.SemaphoreType.DMA((5,)),
-            pltpu.SemaphoreType.DMA((5,)),
+            pltpu.SemaphoreType.DMA((6,)),
+            pltpu.SemaphoreType.DMA((6,)),
         ],
         compiler_params=pltpu.CompilerParams(
             collective_id=0, has_side_effects=True, vmem_limit_bytes=48 << 20

time: 83.1 us -> 83 us (level); the launches traced: 81.5 us -> 82.8 us
  Pallas kernels: 81.3 us -> 82.6 us
    pallas_call x1, Pallas kernels: 78 us -> 79.3 us  [shards(): pl.pallas_call(spread, name='spread', out_shape=kept, in_specs=[anywhere,...]
where the time goes in v6:
time: 83 us; the launch traced here: 82.8 us
  Pallas kernels  82.6 us (100%)
    pallas_call x1, Pallas kernels, shards(): pl.pallas_call(spread, name='spread', out_shape=kept, in_specs=[anywhere,...  79.3 us
    pallas_call x1, Pallas kernels, shards(): pl.pallas_call(finish, name='finish', out_shape=jax.ShapeDtypeStruct((2,...  3.34 us

profile of v6, /device:TPU:1, one launch (start us, length us, event | category | flops | bytes accessed | tf_op | source)
XLA Modules:
  0.0 82.8 jit_solution(8516681672047737029)
XLA Ops:
  0.0 79.3 %spread.1 = (bf16[2,1024,1024]{2,1,0:T(8,128)(2,1)S(1)}, f32[2,256,2560]{2,1,0:T(8,128)S(1)}, bf16[208,1024]{1,0:T(8,128)(2,1)S(1)}, bf16[208,1024]{1,0:T(8,128)(2,1)S(1)}) custom-call(bf16[2048,1024]{1,0:T(8,128)(2,1)} %volt_ref.1, f32[4,512]{1,0:T(4,128)} %taps_ref.1, bf16[2,256,512]{2,1,0:T(8,128)(2,1)} %constant.2.clone.table_ref), custom_call_target="tpu_custom_call" | custom-call | tf_op jit(solution)/shard_map/spread/pallas_call | solution.py:364
  79.3 3.3 %finish.1 = bf16[2,2,1024,1024]{3,2,1,0:T(8,128)(2,1)} custom-call(bf16[2,1024,1024]{2,1,0:T(8,128)(2,1)S(1)} %get-tuple-element.9.vis_ref, f32[2,256,2560]{2,1,0:T(8,128)S(1)} %get-tuple-element.10.sums, bf16[208,1024]{1,0:T(8,128)(2,1)S(1)} %get-tuple-element.11.x_ref, bf16[208,1024]{1,0:T(8,128)(2,1)S(1)} %get-tuple-element.12.y_ref), custom_call_target="tpu_custom_call" | custom-call | tf_op jit(solution)/shard_map/finish/pallas_call | solution.py:394

commit v7 on v6

--- a/solution.py
+++ b/solution.py
@@ -112,12 +112,16 @@
     row, col = lax.axis_index("row"), lax.axis_index("col")
     me = row * 16 + col
     core = col % 2
+    near = []
+    for half in range(2):
+        lanes = pl.ds(half * HALF, HALF)
+        own = frames.at[pl.ds(LATE * POINTS, OWN * POINTS), lanes]
+        near.append(pltpu.make_async_copy(volt_ref.at[:, lanes], own, near_sem.at[half]))
+        near[half].start()
     barrier = pltpu.get_barrier_semaphore()
     for offset in ORDER:
         pl.semaphore_signal(barrier, inc=1, device_id=partner(offset), device_id_type=MESH)
 
-    near = pltpu.make_async_copy(volt_ref, frames.at[pl.ds(LATE * POINTS, OWN * POINTS)], near_sem)
-    near.start()
     padded = jnp.concatenate([taps_ref[...], jnp.zeros((LANES - TAPS, POINTS), jnp.float32)], axis=0)
     for first in range(0, POINTS, LANES):
         columns = padded[:, first : first + LANES].T
@@ -133,11 +137,11 @@
         device_id_type=MESH,
     )
 
-    def filter_frames(outputs, slots):
+    def filter_frames(outputs, slots, half):
         def rows16(step, carry):
             rows = pl.ds(pl.multiple_of(step * 16, 16), 16)
             taps = [jnp.concatenate([weights[tap, rows, :]] * 2, axis=1) for tap in range(TAPS)]
-            for left in range(0, SIGNALS, 256):
+            for left in range(half * HALF, (half + 1) * HALF, 256):
                 lanes = slice(left, left + 256)
                 values = {}
                 for slot in slots:
@@ -154,59 +158,56 @@
 
         lax.fori_loop(0, POINTS // 16, rows16, 0)
 
-    def transform(channel, index, frame):
-        half = index % 2
-        lanes = pl.ds(pl.multiple_of(half * HALF, HALF), HALF)
-        return half, jnp.dot(table_ref[channel], filtered[frame, :, lanes], preferred_element_type=jnp.float32)
-
-    def transform_main(channel):
-        def one(index, carry):
-            frame = index // 2
-            half, spectrum = transform(channel, index, frame)
+    def transform(channel, half, frame):
+        values = filtered[frame, :, half * HALF : (half + 1) * HALF]
+        return jnp.dot(table_ref[channel], values, preferred_element_type=jnp.float32)
+
+    def transform_main(channel, half):
+        def one(frame, carry):
+            spectrum = transform(channel, half, frame)
             for group in range(GROUPS // 2):
                 rows = pl.ds(frame, 2 * DEVICES, stride=OWN)
                 main[half * (GROUPS // 2) + group, rows, :] = spectrum[:, group * LANES : (group + 1) * LANES]
             return carry
 
-        lax.fori_loop(0, 2 * OWN, one, 0)
-
-    def transform_late(channel):
-        def one(index, carry):
-            late = index // 2
-            half, spectrum = transform(channel, index, late + OWN)
+        lax.fori_loop(0, OWN, one, 0)
+
+    def transform_late(channel, half):
+        def one(late, carry):
+            spectrum = transform(channel, half, late + OWN)
             for group in range(GROUPS // 2):
                 rows = pl.ds(half * (GROUPS // 2) + group, 2 * DEVICES, stride=GROUPS)
                 tails[late, rows, :] = spectrum[:, group * LANES : (group + 1) * LANES]
             return carry
 
-        lax.fori_loop(0, 2 * LATE, one, 0)
-
-    def pack_main(channel):
+        lax.fori_loop(0, LATE, one, 0)
+
+    def pack_main(channel, target):
+        rows = pl.ds(pl.multiple_of(target * 8, 8), 8)
+        for group in range(GROUPS // 2):
+            both = jnp.concatenate([main[group, rows, :], main[group + GROUPS // 2, rows, :]], axis=0)
+            outbox[channel, target, :, group * LANES : (group + 1) * LANES] = both.astype(jnp.bfloat16)
+
+    def pack_late(channel, target):
+        rows = pl.ds(pl.multiple_of(target * 16, 16), 16)
+        for late in range(LATE):
+            outbox_late[channel, target, :, late * LANES : (late + 1) * LANES] = tails[late, rows, :].astype(
+                jnp.bfloat16
+            )
+
+    def pack_all(pack, channel):
         def one(target, carry):
-            rows = pl.ds(pl.multiple_of(target * 8, 8), 8)
-            for group in range(GROUPS // 2):
-                both = jnp.concatenate([main[group, rows, :], main[group + GROUPS // 2, rows, :]], axis=0)
-                outbox[channel, target, :, group * LANES : (group + 1) * LANES] = both.astype(jnp.bfloat16)
-            return carry
-
-        lax.fori_loop(0, DEVICES, one, 0, unroll=4)
-
-    def pack_late(channel):
-        def one(target, carry):
-            rows = pl.ds(pl.multiple_of(target * 16, 16), 16)
-            for late in range(LATE):
-                outbox_late[channel, target, :, late * LANES : (late + 1) * LANES] = tails[late, rows, :].astype(
-                    jnp.bfloat16
-                )
-            return carry
-
-        lax.fori_loop(0, DEVICES, one, 0, unroll=4)
+            pack(channel, target)
+            return carry
+
+        lax.fori_loop(0, DEVICES, one, 0, unroll=8)
 
     def send(channel, box, into, place, sem, order=ORDER):
         for offset in order:
             to = partner(offset)
+            target = to[0] * 16 + to[1]
             pltpu.make_async_remote_copy(
-                src_ref=box.at[channel, to[0] * 16 + to[1]],
+                src_ref=box.at[channel, target],
                 dst_ref=into.at[channel, place],
                 send_sem=send_sem.at[sem],
                 recv_sem=recv_sem.at[sem],
@@ -277,39 +278,44 @@
             place = partner(offset + (0,))
             merge(channel, place[0] * 8 + place[1] // 2, slice(index * 16, index * 16 + 16), x_to, y_to)
 
-    near.wait()
-
     @pl.when(core == 0)
     def _():
         frames[0 : LATE * POINTS, :] = jnp.zeros((LATE * POINTS, SIGNALS), jnp.bfloat16)
-        filter_frames(range(OWN), range(OWN + LATE))
-        transform_main(0)
-        pack_main(0)
+        for half in range(2):
+            near[half].wait()
+            filter_frames(range(OWN), range(OWN + LATE), half)
+            transform_main(0, half)
+        pack_all(pack_main, 0)
         pl.semaphore_wait(barrier, len(ORDER))
         halo.start()
         send(0, outbox, inbox, me, 0)
 
     @pl.when(core == 1)
     def _():
-        filter_frames(range(OWN, OWN + LATE), range(OWN, OWN + LATE))
-        transform_late(0)
-        pack_late(0)
+        for half in range(2):
+            near[half].wait()
+            filter_frames(range(OWN, OWN + LATE), range(OWN, OWN + LATE), half)
+            transform_late(0, half)
+        pack_all(pack_late, 0)
         pl.semaphore_wait(barrier, len(ORDER))
         send(0, outbox_late, inbox_late, me // 2, 2)
         inbox_late[0, me // 2] = outbox_late[0, me]
         halo.wait_recv()
-        filter_frames(range(OWN), range(OWN + LATE))
-        transform_main(0)
-        pack_main(0)
+        for half in range(2):
+            filter_frames(range(OWN), range(OWN + LATE), half)
+            transform_main(0, half)
+        pack_all(pack_main, 0)
         send(0, outbox, inbox, me, 0)
-        transform_late(1)
-        pack_late(1)
+        for half in range(2):
+            transform_late(1, half)
+        pack_all(pack_late, 1)
         send(1, outbox_late, inbox_late, me // 2, 3)
         inbox_late[1, me // 2] = outbox_late[1, me]
 
     inbox[0, me] = outbox[0, me]
-    transform_main(1)
-    pack_main(1)
+    for half in range(2):
+        transform_main(1, half)
+    pack_all(pack_main, 1)
     for sends, sem in zip(SENDS, LOT_SEM):
         send(1, outbox, inbox, me, sem, sends)
     inbox[1, me] = outbox[1, me]
@@ -381,7 +387,7 @@
             pltpu.VMEM((GROUPS, 4 * DEVICES, LANES), f32),
             pltpu.VMEM((2 * SPECTRA, SIGNALS), bf16),
             pltpu.VMEM((2 * SPECTRA, SIGNALS), bf16),
-            pltpu.SemaphoreType.DMA(()),
+            pltpu.SemaphoreType.DMA((2,)),
             pltpu.SemaphoreType.DMA((2,)),
             pltpu.SemaphoreType.DMA((6,)),
             pltpu.SemaphoreType.DMA((6,)),

time: 83 us -> 83.3 us (level)
  no operation moved by 1% of the time
where the time goes in v7:
time: 83.3 us; the launch traced here: 83.2 us
  Pallas kernels  83 us (100%)
    pallas_call x1, Pallas kernels, shards(): pl.pallas_call(spread, name='spread', out_shape=kept, in_specs=[anywhere,...  79.7 us
    pallas_call x1, Pallas kernels, shards(): pl.pallas_call(finish, name='finish', out_shape=jax.ShapeDtypeStruct((2,...  3.34 us

profile of v7, /device:TPU:1, one launch (start us, length us, event | category | flops | bytes accessed | tf_op | source)
XLA Modules:
  0.0 83.2 jit_solution(15413596470586429565)
XLA Ops:
  0.0 79.7 %spread.1 = (bf16[2,1024,1024]{2,1,0:T(8,128)(2,1)S(1)}, f32[2,256,2560]{2,1,0:T(8,128)S(1)}, bf16[208,1024]{1,0:T(8,128)(2,1)S(1)}, bf16[208,1024]{1,0:T(8,128)(2,1)S(1)}) custom-call(bf16[2048,1024]{1,0:T(8,128)(2,1)} %volt_ref.1, f32[4,512]{1,0:T(4,128)} %taps_ref.1, bf16[2,256,512]{2,1,0:T(8,128)(2,1)} %constant.2.clone.table_ref), custom_call_target="tpu_custom_call" | custom-call | tf_op jit(solution)/shard_map/spread/pallas_call | solution.py:370
  79.7 3.3 %finish.1 = bf16[2,2,1024,1024]{3,2,1,0:T(8,128)(2,1)} custom-call(bf16[2,1024,1024]{2,1,0:T(8,128)(2,1)S(1)} %get-tuple-element.9.vis_ref, f32[2,256,2560]{2,1,0:T(8,128)S(1)} %get-tuple-element.10.sums, bf16[208,1024]{1,0:T(8,128)(2,1)S(1)} %get-tuple-element.11.x_ref, bf16[208,1024]{1,0:T(8,128)(2,1)S(1)} %get-tuple-element.12.y_ref), custom_call_target="tpu_custom_call" | custom-call | tf_op jit(solution)/shard_map/finish/pallas_call | solution.py:400

commit v8 on v4

--- a/solution.py
+++ b/solution.py
@@ -42,6 +42,7 @@
 
 
 ORDER = send_order()
+NEAR = 84
 
 
 def coordinates():
@@ -54,6 +55,11 @@
     x, y, z = ((own + step) % 4 for own, step in zip(place[:3], offset[:3]))
     core = (place[3] + offset[3]) % 2
     return (x % 2) * 4 + y, z * 4 + (x // 2) * 2 + core
+
+
+def entry(place):
+    row, col = place
+    return (col // 2 % 2) * 2 + row // 4 + row % 4 + 2 * (col // 4)
 
 
 def fourier_rows():
@@ -96,12 +102,12 @@
     row, col = lax.axis_index("row"), lax.axis_index("col")
     me = row * 16 + col
     core = col % 2
+    near = pltpu.make_async_copy(volt_ref, frames.at[pl.ds(LATE * POINTS, OWN * POINTS)], near_sem)
+    near.start()
     barrier = pltpu.get_barrier_semaphore()
     for offset in ORDER:
         pl.semaphore_signal(barrier, inc=1, device_id=partner(offset), device_id_type=MESH)
 
-    near = pltpu.make_async_copy(volt_ref, frames.at[pl.ds(LATE * POINTS, OWN * POINTS)], near_sem)
-    near.start()
     padded = jnp.concatenate([taps_ref[...], jnp.zeros((LANES - TAPS, POINTS), jnp.float32)], axis=0)
     for first in range(0, POINTS, LANES):
         columns = padded[:, first : first + LANES].T
@@ -186,17 +192,19 @@
 
         lax.fori_loop(0, DEVICES, one, 0, unroll=4)
 
-    def send(channel, box, into, place, sem):
-        for offset in ORDER:
-            to = partner(offset)
-            pltpu.make_async_remote_copy(
-                src_ref=box.at[channel, to[0] * 16 + to[1]],
-                dst_ref=into.at[channel, place],
-                send_sem=send_sem.at[sem],
-                recv_sem=recv_sem.at[sem],
-                device_id=to,
-                device_id_type=MESH,
-            ).start()
+    def send_to(channel, box, into, place, sem, to):
+        pltpu.make_async_remote_copy(
+            src_ref=box.at[channel, to[0] * 16 + to[1]],
+            dst_ref=into.at[channel, place],
+            send_sem=send_sem.at[sem],
+            recv_sem=recv_sem.at[sem],
+            device_id=to,
+            device_id_type=MESH,
+        ).start()
+
+    def send(channel, box, into, place, sem, order=ORDER):
+        for offset in order:
+            send_to(channel, box, into, place, sem, partner(offset))
 
     def arrived(channel):
         most = inbox.at[channel, pl.ds(0, DEVICES - 1)]
@@ -283,7 +291,16 @@
     inbox[0, me] = outbox[0, me]
     transform_main(1)
     pack_main(1)
-    send(1, outbox, inbox, me, 1)
+    send(1, outbox, inbox, me, 1, ORDER[:NEAR])
+    for later in range(2):
+        for offset in ORDER[NEAR:]:
+            mirrored = tuple((-step) % 4 for step in offset[:3]) + offset[3:]
+            if mirrored > offset or (mirrored == offset and not later):
+                one, two = partner(offset), partner(mirrored)
+                swap = (entry(one) > entry(two)).astype(jnp.int32)
+                swap = 1 - swap if later else swap
+                to = tuple(first + swap * (second - first) for first, second in zip(one, two))
+                send_to(1, outbox, inbox, me, 1, to)
     inbox[1, me] = outbox[1, me]
 
     arrived(0)

time: 82.8 us -> 81.6 us (0.986)
  Pallas kernels: 82.7 us -> 81.3 us
    pallas_call x1, Pallas kernels: 78.5 us -> 77.1 us  [shards(): pl.pallas_call(spread, name='spread', out_shape=kept, in_specs=[anywhere,...]
where the time goes in v8:
time: 81.6 us; the launch traced here: 81.5 us
  Pallas kernels  81.3 us (100%)
    pallas_call x1, Pallas kernels, shards(): pl.pallas_call(spread, name='spread', out_shape=kept, in_specs=[anywhere,...  77.1 us
    pallas_call x1, Pallas kernels, shards(): pl.pallas_call(finish, name='finish', out_shape=jax.ShapeDtypeStruct((2,...  4.17 us

profile of v8, /device:TPU:1, one launch (start us, length us, event | category | flops | bytes accessed | tf_op | source)
XLA Modules:
  0.0 81.5 jit_solution(4017285286211684457)
XLA Ops:
  0.0 77.1 %spread.1 = (bf16[2,1024,1024]{2,1,0:T(8,128)(2,1)S(1)}, bf16[1024,1024]{1,0:T(8,128)(2,1)S(1)}, bf16[1024,1024]{1,0:T(8,128)(2,1)S(1)}) custom-call(bf16[2048,1024]{1,0:T(8,128)(2,1)} %volt_ref.1, f32[4,512]{1,0:T(4,128)} %taps_ref.1, bf16[2,256,512]{2,1,0:T(8,128)(2,1)} %constant.2.clone.table_ref), custom_call_target="tpu_custom_call" | custom-call | tf_op jit(solution)/shard_map/spread/pallas_call | solution.py:341
  77.1 4.2 %finish.1 = bf16[2,2,1024,1024]{3,2,1,0:T(8,128)(2,1)} custom-call(bf16[2,1024,1024]{2,1,0:T(8,128)(2,1)S(1)} %get-tuple-element.8.vis_ref, bf16[1024,1024]{1,0:T(8,128)(2,1)S(1)} %get-tuple-element.9.x_ref, bf16[1024,1024]{1,0:T(8,128)(2,1)S(1)} %get-tuple-element.10.y_ref), custom_call_target="tpu_custom_call" | custom-call | tf_op jit(solution)/shard_map/finish/pallas_call | solution.py:369
